TPU v7x, 128 devices: a whole 4x4x4 slice. The times are simulated.
128 devices in a mesh: ctx: 8 (over y_lo, x), wsh: 16 (over z, y_hi, core).
Axes of the slice: x: 4, y: 4 (y_hi: 2, y_lo: 2; y = y_hi * 2 + y_lo), z: 4, core: 2. Of those that a mesh axis runs over, the one named last changes fastest.
Arguments:
- tokens: bfloat16 [16, 1024, 1024], P('wsh', 'ctx'), may hold values from -6 to 6
- gain_attn: bfloat16 [1024], P('wsh'), may hold values from 0.5 to 1.5
- w_query: bfloat16 [1024, 1024], P('wsh'), may hold values from -0.1875 to 0.1875
- w_key: bfloat16 [1024, 512], P('wsh'), may hold values from -0.1875 to 0.1875
- w_value: bfloat16 [1024, 512], P('wsh'), may hold values from -0.1875 to 0.1875
- w_output: bfloat16 [1024, 1024], P('wsh'), may hold values from -1 to 1
- gain_moe: bfloat16 [1024], P('wsh'), may hold values from 0.5 to 1.5
- w_router: bfloat16 [1024, 32], P('wsh'), may hold values from -0.09375 to 0.09375
- w_in: bfloat16 [32, 1024, 1024], P('wsh'), may hold values from -0.1875 to 0.1875
- w_out: bfloat16 [32, 1024, 512], P('wsh'), may hold values from -1 to 1
- routes: int32 [16, 8, 128, 8], P('wsh', 'ctx'), may hold values from 0 to 31, all different within a row; in each aligned block of 128 rows (0 to 127, 128 to 255, ..., all dimensions but the last counted through in order) at most 64 rows name the same one
- cotangent: bfloat16 [16, 1024, 1024], P('wsh', 'ctx'), may hold values from -6 to 6
Outputs:
- output: bfloat16 [16, 1024, 1024], P('wsh', 'ctx')
- tokens_grad: bfloat16 [16, 1024, 1024], P('wsh', 'ctx')
- gain_attn_grad: float32 [1024], P('wsh')
- w_query_grad: float32 [1024, 1024], P('wsh')
- w_key_grad: float32 [1024, 512], P('wsh')
- w_value_grad: float32 [1024, 512], P('wsh')
- w_output_grad: float32 [1024, 1024], P('wsh')
- gain_moe_grad: float32 [1024], P('wsh')
- w_router_grad: float32 [1024, 32], P('wsh')
- w_in_grad: float32 [32, 1024, 1024], P('wsh', 'ctx')
- w_out_grad: float32 [32, 1024, 512], P('wsh', 'ctx')
Inputs may be any that keep to these rules, and one draw needn't show every extreme that they name: `routes`: each row names 8 different experts; in the rows of one device (aligned blocks of 128 rows in array order) no expert is named more than 64 times, a bound that some block reaches.
All inputs are finite; a program needn't handle non-finite values.
Results may differ from a plain program's by a relative error of at most 0.025.
Values may be sent and summed in bfloat16 or wider, within the bound.
A program may use at most 192 MiB of HBM per device.

v0:
```python
import math

import jax
import jax.numpy as jnp
from jax import lax
from jax.sharding import PartitionSpec as P

DH = 64


epsilon = 1e-05
rope_base = 10000.0
masked_score = -1e30
full_precision = lax.Precision.HIGHEST


def in_one_piece(arrays, axis, dim, along):
    columns = [a.reshape(*a.shape[:along], -1) for a in arrays]
    both = jnp.concatenate(columns, axis=along)
    filled, at, done = (lax.all_gather(both, axis, axis=dim, tiled=True), 0, [])
    for a, column in zip(arrays, columns):
        section = filled[..., at : at + column.shape[along]]
        done.append(section.reshape(*section.shape[:along], *a.shape[along:]))
        at += column.shape[along]
    return tuple(done)


def sent_together(arrays, axis, dim, along):
    widths = [a.shape[along] for a in arrays]
    both = jnp.concatenate(arrays, axis=along)
    filled = lax.all_gather(both, axis, axis=dim, tiled=True)
    return tuple(jnp.split(filled, [sum(widths[:k]) for k in range(1, len(widths))], axis=along))


def sent_together_2(arrays, axis, dim, along):
    widths = [math.prod(a.shape[along:]) for a in arrays]
    both = jnp.concatenate(
        [a.reshape(*a.shape[:along], w) for a, w in zip(arrays, widths)], axis=along
    )
    filled = lax.psum_scatter(both, axis, scatter_dimension=dim, tiled=True)
    blocks = jnp.split(filled, [sum(widths[:k]) for k in range(1, len(widths))], axis=along)
    return tuple(
        (b.reshape(*filled.shape[:along], *a.shape[along:]) for a, b in zip(arrays, blocks))
    )


def from_everyone(shard, axis):
    copies = jnp.broadcast_to(shard, (lax.axis_size(axis), *shard.shape))
    return lax.all_to_all(copies, axis, split_axis=0, concat_axis=0, tiled=True)


def over_copies(shard, axis):
    everything = from_everyone(shard, axis)
    return jnp.sum(everything.astype(jnp.float32), axis=0)


def in_one_piece_2(arrays, axis, dim, along):
    ends, at = ([], 0)
    for a in arrays[:-1]:
        at += a.shape[along]
        ends.append(at)
    both = jnp.concatenate(arrays, axis=along)
    return tuple(
        jnp.split(lax.psum_scatter(both, axis, scatter_dimension=dim, tiled=True), ends, axis=along)
    )


def rms_scale(token_rows):
    return lax.rsqrt(jnp.mean(token_rows * token_rows, -1, keepdims=True) + epsilon)


def norm_back(grad_normed, token_rows, scale):
    mean_term = jnp.mean(grad_normed * token_rows, -1, keepdims=True)
    return scale * grad_normed - token_rows * scale * scale * scale * mean_term


def rope_tables(positions, head_width):
    half_width = head_width // 2
    frequencies = rope_base ** (-jnp.arange(half_width, dtype=jnp.float32) * 2.0 / head_width)
    angles = positions[:, None] * frequencies[None, :]
    cosine_table = jnp.cos(angles)
    sine_table = jnp.sin(angles)
    return (
        jnp.concatenate([cosine_table, cosine_table], -1),
        jnp.concatenate([sine_table, sine_table], -1),
    )


def rotate(values, cosine_table, sine_table):
    half_width = values.shape[-1] // 2
    turned = jnp.concatenate([-values[..., half_width:], values[..., :half_width]], -1)
    return values * cosine_table[:, None, :] + turned * sine_table[:, None, :]


def unrotate(gradients, cosine_table, sine_table):
    half_width = gradients.shape[-1] // 2
    scaled = gradients * sine_table[:, None, :]
    turned = jnp.concatenate([scaled[..., half_width:], -scaled[..., :half_width]], -1)
    return gradients * cosine_table[:, None, :] + turned


def attend_scores(queries, key_rows, first_pos):
    raw_scores = jnp.einsum("tgrd,jgd->grtj", queries, key_rows, preferred_element_type=jnp.float32)
    scores = raw_scores * DH ** (-0.5)
    query_pos = first_pos + jnp.arange(queries.shape[0], dtype=jnp.int32)
    key_pos = jnp.arange(key_rows.shape[0], dtype=jnp.int32)
    visible = key_pos[None, :] <= query_pos[:, None]
    return jnp.where(visible, scores, masked_score)


def slot_of(chosen_ids, expert_count, capacity):
    flat_ids = chosen_ids.reshape(-1)
    matches = (flat_ids[:, None] == jnp.arange(expert_count, dtype=jnp.int32)[None, :]).astype(
        jnp.int32
    )
    earlier = jnp.cumsum(matches, 0) - matches
    return flat_ids * capacity + jnp.sum(earlier * matches, 1)


def local(
    tokens,
    gain_attn,
    w_query,
    w_key,
    w_value,
    w_output,
    gain_moe,
    w_router,
    w_in,
    w_out,
    routes,
    cotangent,
):
    seq_count, length, model_width = tokens.shape
    full_length = length * lax.axis_size("ctx")
    first_pos = lax.axis_index("ctx") * length
    token_rows = tokens.astype(jnp.float32).reshape(seq_count * length, model_width)
    wq, wk, wv, wo, wr, gain_one, gain_two = in_one_piece(
        (w_query, w_key, w_value, w_output, w_router, gain_attn, gain_moe), "wsh", 0, 1
    )
    head_count = wq.shape[1] // DH
    kv_heads = wk.shape[1] // DH
    group_size = head_count // kv_heads
    kv_width = kv_heads * DH
    scale_attn = rms_scale(token_rows)
    normed_attn = (token_rows * scale_attn * gain_one).astype(jnp.bfloat16)
    query_pre = jnp.dot(normed_attn, wq, preferred_element_type=jnp.float32)
    key_pre = jnp.dot(normed_attn, wk, preferred_element_type=jnp.float32)
    value_pre = jnp.dot(normed_attn, wv, preferred_element_type=jnp.float32)
    positions = (first_pos + jnp.arange(length, dtype=jnp.int32)).astype(jnp.float32)
    cosine_table, sine_table = rope_tables(positions, DH)
    queries = rotate(
        query_pre.reshape(seq_count, length, head_count, DH), cosine_table, sine_table
    ).astype(jnp.bfloat16)
    key_rows = rotate(key_pre.reshape(seq_count, length, kv_heads, DH), cosine_table, sine_table)
    key_rows = key_rows.astype(jnp.bfloat16).reshape(seq_count, length, kv_width)
    value_rows = value_pre.astype(jnp.bfloat16).reshape(seq_count, length, kv_width)
    all_keys, all_values = sent_together((key_rows, value_rows), "ctx", 1, 0)
    grouped = queries.reshape(seq_count, length, kv_heads, group_size, DH)

    def forward_one(operand):
        query_seq, key_seq, value_seq = operand
        key_seq = key_seq.reshape(full_length, kv_heads, DH)
        value_seq = value_seq.reshape(full_length, kv_heads, DH)
        scores = attend_scores(query_seq, key_seq, first_pos)
        row_max = jnp.max(scores, -1, keepdims=True)
        logsum = row_max + jnp.log(jnp.sum(jnp.exp(scores - row_max), -1, keepdims=True))
        attention = jnp.exp(scores - logsum).astype(jnp.bfloat16)
        mixed = jnp.einsum(
            "grtj,jgd->tgrd", attention, value_seq, preferred_element_type=jnp.float32
        )
        return (mixed, logsum)

    mixed, logsums = lax.map(forward_one, (grouped, all_keys, all_values))
    merged = mixed.astype(jnp.bfloat16).reshape(seq_count * length, head_count * DH)
    residual = token_rows + jnp.dot(merged, wo, preferred_element_type=jnp.float32)
    scale_moe = rms_scale(residual)
    normed_moe = (residual * scale_moe * gain_two).astype(jnp.bfloat16)
    logits = jnp.dot(normed_moe, wr, preferred_element_type=jnp.float32)
    expert_count = wr.shape[1]
    top_count = routes.shape[-1]
    chosen_ids = routes.reshape(-1, top_count)
    chosen = jnp.take_along_axis(logits, chosen_ids, 1)
    row_max = jnp.max(chosen, -1, keepdims=True)
    raised = jnp.exp(chosen - row_max)
    gate_weights = raised / jnp.sum(raised, -1, keepdims=True)
    capacity = chosen_ids.shape[0] // 2
    slot_index = slot_of(chosen_ids, expert_count, capacity)
    peer_count = lax.axis_size("wsh")
    local_count = expert_count // peer_count
    copies = jnp.repeat(normed_moe, top_count, axis=0)
    outgoing = (
        jnp.zeros((expert_count * capacity, model_width), jnp.bfloat16).at[slot_index].set(copies)
    )
    outgoing = outgoing.reshape(peer_count, local_count, capacity, model_width)
    arrived = lax.all_to_all(outgoing, "wsh", split_axis=0, concat_axis=0, tiled=True)
    projected = jnp.einsum("sjcd,jfd->sjcf", arrived, w_in, preferred_element_type=jnp.float32)
    hidden_units = projected.shape[-1] // 2
    hidden = (jax.nn.silu(projected[..., :hidden_units]) * projected[..., hidden_units:]).astype(
        jnp.bfloat16
    )
    produced = jnp.einsum(
        "sjcf,jdf->sjcd", hidden, w_out, preferred_element_type=jnp.float32
    ).astype(jnp.bfloat16)
    returned = lax.all_to_all(produced, "wsh", split_axis=0, concat_axis=0, tiled=True)
    returned, arrived, projected, hidden = (returned, arrived, projected, hidden)
    picked = returned.reshape(expert_count * capacity, model_width)[slot_index].reshape(
        -1, top_count, model_width
    )
    expert_sum = jnp.sum(gate_weights[..., None] * picked, 1)
    output = (residual + expert_sum).astype(jnp.bfloat16).reshape(seq_count, length, model_width)
    grad_out = cotangent.astype(jnp.float32).reshape(-1, model_width)
    grad_gates = jnp.sum(grad_out[:, None, :] * picked, -1)
    grad_picked = (gate_weights[..., None] * grad_out[:, None, :]).astype(jnp.bfloat16)
    grad_send = (
        jnp.zeros((expert_count * capacity, model_width), jnp.bfloat16)
        .at[slot_index]
        .set(grad_picked.reshape(-1, model_width))
    )
    grad_send = grad_send.reshape(peer_count, local_count, capacity, model_width)
    grad_arrived = lax.all_to_all(grad_send, "wsh", split_axis=0, concat_axis=0, tiled=True)
    hidden_units = projected.shape[-1] // 2
    gate_part = projected[..., :hidden_units]
    up_part = projected[..., hidden_units:]
    grad_w_out = jnp.einsum(
        "sjcd,sjcf->jdf", grad_arrived, hidden, preferred_element_type=jnp.float32
    )
    grad_hidden = jnp.einsum(
        "sjcd,jdf->sjcf", grad_arrived, w_out, preferred_element_type=jnp.float32
    )
    sigmoid_gate = jax.nn.sigmoid(gate_part)
    grad_gate = grad_hidden * up_part * sigmoid_gate * (1.0 + gate_part * (1.0 - sigmoid_gate))
    grad_up = grad_hidden * gate_part * sigmoid_gate
    grad_act = jnp.concatenate([grad_gate, grad_up], -1).astype(jnp.bfloat16)
    grad_w_in = jnp.einsum("sjcf,sjcd->jfd", grad_act, arrived, preferred_element_type=jnp.float32)
    grad_copy = jnp.einsum(
        "sjcf,jfd->sjcd", grad_act, w_in, preferred_element_type=jnp.float32
    ).astype(jnp.bfloat16)
    grad_back = lax.all_to_all(grad_copy, "wsh", split_axis=0, concat_axis=0, tiled=True)
    grad_copies = grad_back.reshape(expert_count * capacity, model_width)[slot_index]
    grad_normed_moe = jnp.sum(
        grad_copies.reshape(-1, top_count, model_width).astype(jnp.float32), 1
    )
    inner_sum = jnp.sum(gate_weights * grad_gates, -1, keepdims=True)
    grad_chosen = gate_weights * (grad_gates - inner_sum)
    matches = (chosen_ids[..., None] == jnp.arange(expert_count, dtype=jnp.int32)).astype(
        jnp.float32
    )
    grad_logits = jnp.sum(matches * grad_chosen[..., None], 1)
    grad_w_router = jnp.dot(normed_moe.astype(jnp.float32).T, grad_logits, precision=full_precision)
    grad_normed_moe = grad_normed_moe + jnp.dot(
        grad_logits, wr.astype(jnp.float32).T, precision=full_precision
    )
    grad_gain_moe = jnp.sum(grad_normed_moe * residual * scale_moe, 0)
    grad_mid = grad_out + norm_back(grad_normed_moe * gain_two, residual, scale_moe)
    grad_branch = grad_mid.astype(jnp.bfloat16)
    grad_w_output = jnp.dot(merged.T, grad_branch, preferred_element_type=jnp.float32)
    grad_merged = jnp.dot(grad_branch, wo.T, preferred_element_type=jnp.float32).astype(
        jnp.bfloat16
    )
    grad_mixed = grad_merged.reshape(seq_count, length, kv_heads, group_size, DH)
    keys_back, values_back = (all_keys, all_values)

    def backward_one(operand):
        query_seq, key_seq, value_seq, logsum, grad_seq = operand
        key_seq = key_seq.reshape(full_length, kv_heads, DH)
        value_seq = value_seq.reshape(full_length, kv_heads, DH)
        scores = attend_scores(query_seq, key_seq, first_pos)
        attention = jnp.exp(scores - logsum)
        attention_low = attention.astype(jnp.bfloat16)
        grad_probs = jnp.einsum(
            "tgrd,jgd->grtj", grad_seq, value_seq, preferred_element_type=jnp.float32
        )
        inner_dot = jnp.sum(attention * grad_probs, -1, keepdims=True)
        grad_raw = (attention * (grad_probs - inner_dot) * DH ** (-0.5)).astype(jnp.bfloat16)
        grad_query = jnp.einsum(
            "grtj,jgd->tgrd", grad_raw, key_seq, preferred_element_type=jnp.float32
        )
        return (grad_query, grad_raw, attention_low)

    grad_queries, grad_raws, attention_all = lax.map(
        backward_one, (grouped, keys_back, values_back, logsums, grad_mixed)
    )
    count = length * lax.axis_size("ctx")
    grad_key = jnp.einsum(
        "sgrtj,stgrd->jsgd", grad_raws, grouped, preferred_element_type=jnp.float32
    )
    grad_value = jnp.einsum(
        "sgrtj,stgrd->jsgd", attention_all, grad_mixed, preferred_element_type=jnp.float32
    )
    key_grads = (
        lax.psum_scatter(
            jnp.concatenate(
                [
                    grad_key.reshape(count, seq_count, kv_width),
                    grad_value.reshape(count, seq_count, kv_width),
                ],
                -1,
            ).astype(jnp.bfloat16),
            "ctx",
            scatter_dimension=0,
            tiled=True,
        )
        .astype(jnp.float32)
        .transpose(1, 0, 2)
    )
    grad_keys = unrotate(
        key_grads[..., :kv_width].reshape(seq_count, length, kv_heads, DH), cosine_table, sine_table
    )
    grad_keys = grad_keys.astype(jnp.bfloat16).reshape(-1, kv_width)
    grad_values = key_grads[..., kv_width:].astype(jnp.bfloat16).reshape(-1, kv_width)
    grad_q = unrotate(
        grad_queries.reshape(seq_count, length, head_count, DH), cosine_table, sine_table
    )
    grad_q = grad_q.astype(jnp.bfloat16).reshape(-1, head_count * DH)
    grad_w_query = jnp.dot(normed_attn.T, grad_q, preferred_element_type=jnp.float32)
    grad_w_key = jnp.dot(normed_attn.T, grad_keys, preferred_element_type=jnp.float32)
    grad_w_value = jnp.dot(normed_attn.T, grad_values, preferred_element_type=jnp.float32)
    grad_normed_attn = jnp.dot(grad_q, wq.T, preferred_element_type=jnp.float32)
    grad_normed_attn = grad_normed_attn + jnp.dot(
        grad_keys, wk.T, preferred_element_type=jnp.float32
    )
    grad_normed_attn = grad_normed_attn + jnp.dot(
        grad_values, wv.T, preferred_element_type=jnp.float32
    )
    grad_gain_attn = jnp.sum(grad_normed_attn * token_rows * scale_attn, 0)
    grad_rows = grad_mid + norm_back(grad_normed_attn * gain_one, token_rows, scale_attn)
    tokens_grad = grad_rows.astype(jnp.bfloat16).reshape(seq_count, length, model_width)
    shares = tuple(
        (
            part.astype(jnp.float32)
            for part in sent_together_2(
                (
                    grad_w_query.astype(jnp.bfloat16),
                    grad_w_key.astype(jnp.bfloat16),
                    grad_w_value.astype(jnp.bfloat16),
                    grad_w_output.astype(jnp.bfloat16),
                    grad_w_router.astype(jnp.bfloat16),
                    grad_gain_attn.astype(jnp.bfloat16),
                    grad_gain_moe.astype(jnp.bfloat16),
                ),
                "wsh",
                0,
                1,
            )
        )
    )
    (
        share_query,
        share_key,
        share_value,
        share_output,
        share_router,
        share_gain_attn,
        share_gain_moe,
    ) = (
        over_copies(shares[0].astype(jnp.bfloat16), "ctx").astype(jnp.float32),
        over_copies(shares[1].astype(jnp.bfloat16), "ctx").astype(jnp.float32),
        over_copies(shares[2].astype(jnp.bfloat16), "ctx").astype(jnp.float32),
        over_copies(shares[3].astype(jnp.bfloat16), "ctx").astype(jnp.float32),
        over_copies(shares[4].astype(jnp.bfloat16), "ctx").astype(jnp.float32),
        over_copies(shares[5].astype(jnp.bfloat16), "ctx").astype(jnp.float32),
        over_copies(shares[6].astype(jnp.bfloat16), "ctx").astype(jnp.float32),
    )
    expert_in, expert_out = tuple(
        (
            part.astype(jnp.float32)
            for part in in_one_piece_2(
                (grad_w_in.astype(jnp.bfloat16), grad_w_out.astype(jnp.bfloat16)), "ctx", 1, 2
            )
        )
    )
    return (
        output,
        tokens_grad,
        share_gain_attn,
        share_query,
        share_key,
        share_value,
        share_output,
        share_gain_moe,
        share_router,
        expert_in,
        expert_out,
    )


def solution(mesh):
    return jax.shard_map(
        local,
        mesh=mesh,
        in_specs=(
            P("wsh", "ctx", None),
            P("wsh"),
            P("wsh", None),
            P("wsh", None),
            P("wsh", None),
            P("wsh", None),
            P("wsh"),
            P("wsh", None),
            P("wsh", None, None),
            P("wsh", None, None),
            P("wsh", "ctx", None, None),
            P("wsh", "ctx", None),
        ),
        out_specs=(
            P("wsh", "ctx", None),
            P("wsh", "ctx", None),
            P("wsh"),
            P("wsh", None),
            P("wsh", None),
            P("wsh", None),
            P("wsh", None),
            P("wsh"),
            P("wsh", None),
            P("wsh", "ctx", None),
            P("wsh", "ctx", None),
        ),
        check_vma=False,
    )
```

profile of v0, /device:TPU:2, one launch (start us, length us, event | category | flops | bytes accessed | tf_op | source)
XLA Modules:
  0.0 745.0 jit_solution(3150493172657001133)
XLA Ops:
  13.8 65.7 %all-gather.3.cloned.1.call-done = bf16[1024,3106]{1,0:T(8,128)(2,1)} async-done(((bf16[64,3106]{1,0:T(8,128)(2,1)}), bf16[1024,3106]{1,0:T(8,128)(2,1)}) %all-gather.3.cloned.1.call-update) | async-done | bytes 6361104 | tf_op jit(solution)/shard_map/all_gather | solution.py:20
  87.5 9.0 %reduce-window.6 = s32[32,8,128]{2,1,0:T(8,128)S(1)} reduce-window(s32[32,8,128]{2,1,0:T(8,128)S(1)} %fusion.104, s32[]{:T(128)} %constant.98.clone.1), window={size=1x1x128 pad=0_0x0_0x127_0}, to_apply=%region_6.7 | reduce-window | flops 4161536 | bytes 262148 | tf_op jit(solution)/shard_map/reduce-window
  102.0 22.2 %all-gather.5.cloned.1.call-done = bf16[2,1024,512]{2,1,0:T(8,128)(2,1)} async-done(((bf16[2,128,512]{2,1,0:T(8,128)(2,1)}), bf16[2,1024,512]{2,1,0:T(8,128)(2,1)}) %all-gather.5.cloned.1.call-update) | async-done | bytes 2097168 | tf_op jit(solution)/shard_map/all_gather | solution.py:31
  140.4 8.2 %scatter_custom_fusion = bf16[2048,1024]{1,0:T(8,128)(2,1)} fusion(s32[1024]{0:T(1024)S(1)} %bitcast.375, bf16[]{:T(256)} %constant.102.clone.1, bf16[128,1024]{1,0:T(8,128)(2,1)S(1)} %multiply_convert_fusion.1), kind=kCustom, calls=%fused_computation.54 | custom fusion | bytes 4456450 | tf_op jit(solution)/shard_map/scatter | solution.py:193
  148.7 6.6 all-to-all-start
  157.8 7.0 gather_fusion.2
  170.8 8.3 %scatter_custom_fusion.1 = bf16[2048,1024]{1,0:T(8,128)(2,1)} fusion(s32[1024]{0:T(1024)S(1)} %bitcast.376, f32[128,1024]{1,0:T(8,128)S(1)} %bitcast_convert_fusion.4, f32[1024]{0:T(1024)S(1)} %exponential_divide_fusion, bf16[]{:T(256)} %constant.102.clone.1), kind=kCustom, calls=%fused_computation.48 | custom fusion | flops 2097152 | bytes 4722690 | tf_op jit(solution)/shard_map/scatter | solution.py:218
  179.1 28.0 %all-to-all-done = bf16[16,2,64,1024]{3,2,1,0:T(8,128)(2,1)} async-done(((bf16[16,2,64,1024]{3,2,1,0:T(8,128)(2,1)}), bf16[16,2,64,1024]{3,2,1,0:T(8,128)(2,1)}, u32[]{:S(2)}, u32[]{:S(2)}) %all-to-all-start) | async-done | bytes 4194336 | tf_op jit(solution)/shard_map/all_to_all | solution.py:196
  207.1 5.0 all-to-all-start.2
  212.1 11.4 %fusion.23 = f32[16,2,64,1024]{3,2,0,1:T(8,128)} fusion(bf16[2,1024,1024]{2,1,0:T(8,128)(2,1)} %param.20, bf16[16,2,64,1024]{3,2,1,0:T(8,128)(2,1)} %all-to-all-done), kind=kOutput, calls=%fused_computation.47 | convolution fusion | flops 4294967296 | bytes 16777216 | tf_op jit(solution)/shard_map/sjcd,jfd->sjcf/dot_general | solution.py:197
  223.5 40.5 %all-to-all-done.2 = bf16[16,2,64,1024]{3,2,1,0:T(8,128)(2,1)} async-done(((bf16[16,2,64,1024]{3,2,1,0:T(8,128)(2,1)}), bf16[16,2,64,1024]{3,2,1,0:T(8,128)(2,1)}, u32[]{:S(2)}, u32[]{:S(2)}) %all-to-all-start.2) | async-done | bytes 4194336 | tf_op jit(solution)/shard_map/all_to_all | solution.py:221
  263.9 8.9 %fusion.14 = (bf16[16,2,64,512]{3,2,0,1:T(8,128)(2,1)S(1)}, bf16[16,2,64,512]{3,2,0,1:T(8,128)(2,1)S(1)}, bf16[16,2,64,512]{3,2,0,1:T(8,128)(2,1)}) fusion(f32[16,2,64,1024]{3,2,0,1:T(8,128)} %fusion.23, bf16[2,1024,512]{2,1,0:T(8,128)(2,1)S(1)} %copy-done, bf16[16,2,64,1024]{3,2,1,0:T(8,128)(2,1)} %all-to-all-done.2), kind=kOutput, calls=%fused_computation.33 | convolution fusion | flops 2164260864 | bytes 20971520 | tf_op jit(solution)/shard_map/sjcd,jdf->sjcf/dot_general | solution.py:228
  272.8 4.7 convert_bitcast_fusion
  291.1 45.3 %all-to-all-done.3 = bf16[16,2,64,1024]{3,2,1,0:T(8,128)(2,1)} async-done(((bf16[16,2,64,1024]{3,2,1,0:T(8,128)(2,1)}), bf16[16,2,64,1024]{3,2,1,0:T(8,128)(2,1)}, u32[]{:S(2)}, u32[]{:S(2)}) %all-to-all-start.3) | async-done | bytes 4194336 | tf_op jit(solution)/shard_map/all_to_all | solution.py:239
  341.9 7.7 %gather_fusion.1 = bf16[1024,1024]{1,0:T(8,128)(2,1)S(1)} fusion(bf16[2048,1024]{1,0:T(8,128)(2,1)} %bitcast.47, s32[1024]{0:T(1024)S(1)} %broadcast_clamp_fusion), kind=kCustom, calls=%fused_computation.1 | custom fusion | bytes 4198400 | tf_op jit(solution)/shard_map/gather | solution.py:240
  351.8 40.9 %all-to-all-done.1 = bf16[16,2,64,1024]{3,2,1,0:T(8,128)(2,1)} async-done(((bf16[16,2,64,1024]{3,2,1,0:T(8,128)(2,1)}), bf16[16,2,64,1024]{3,2,1,0:T(8,128)(2,1)}, u32[]{:S(2)}, u32[]{:S(2)}) %all-to-all-start.1) | async-done | bytes 4194336 | tf_op jit(solution)/shard_map/all_to_all | solution.py:205
  392.8 7.7 %gather_fusion = bf16[1024,1024]{1,0:T(8,128)(2,1)S(1)} fusion(bf16[2048,1024]{1,0:T(8,128)(2,1)} %bitcast.36, s32[1024]{0:T(1024)S(1)} %broadcast_clamp_fusion), kind=kCustom, calls=%fused_computation | custom fusion | bytes 4198400 | tf_op jit(solution)/shard_map/gather | solution.py:207
  409.8 6.4 bitcast_convert_fusion.2
  420.7 15.0 %bitcast_convert_fusion.3 = bf16[8,64,1024]{2,1,0:T(8,128)(2,1)} fusion(bf16[128,8,2,64]{0,3,2,1:T(8,128)(2,1)S(1)} %copy-done.16, f32[8,1024,128,2]{2,1,3,0:T(8,128)} %fusion.142, f32[8,1024,128,2]{2,1,3,0:T(8,128)} %copy-done.2, f32[8,2,128]{2,1,0:T(2,128)S(1)} %bitcast.380, pred[128,1024]{0,1:T(8,128)(4,1)S(1)} %copy-done.13), kind=kOutput, calls=%fused_computation.51 | convolution fusion | flops 292031488 | bytes 18227200 | tf_op jit(solution)/shard_map/sgrtj,stgrd->jsgd/dot_general | solution.py:285
  440.1 16.5 %fusion.53 = f32[8,64,2,128]{3,1,2,0:T(8,128)S(1)} fusion(bf16[1024,8,64,1]{0,2,3,1:T(8,128)(2,1)} %bitcast.344, f32[8,1024,128,2]{2,1,3,0:T(8,128)} %fusion.142, f32[8,1024,128,2]{2,1,3,0:T(8,128)} %copy-done.2, f32[8,2,128]{2,1,0:T(2,128)S(1)} %bitcast.381, pred[128,1024]{0,1:T(8,128)(4,1)} %iota_compare_fusion), kind=kOutput, calls=%fused_computation.75 | convolution fusion | flops 291507200 | bytes 18489344 | tf_op jit(solution)/shard_map/while/body/eval_jaxpr/grtj,jgd->tgrd/dot_general | solution.py:276
  464.6 13.2 %reduce-scatter.10.cloned.1.call-done = bf16[128,1024]{1,0:T(8,128)(2,1)} async-done(((bf16[1024,1024]{1,0:T(8,128)(2,1)}), bf16[128,1024]{1,0:T(8,128)(2,1)}) %reduce-scatter.10.cloned.1.call-update) | async-done | bytes 262160
  486.4 26.4 %concatenate.100 = bf16[1024,3106]{0,1:T(8,128)(2,1)} concatenate(bf16[1024,1024]{0,1:T(8,128)(2,1)S(1)} %convolution_convert_fusion, bf16[1024,512]{0,1:T(8,128)(2,1)} %convolution_convert_fusion.3, bf16[1024,512]{0,1:T(8,128)(2,1)} %convolution_convert_fusion.2, bf16[1024,1024]{0,1:T(8,128)(2,1)} %convolution_convert_fusion.1, bf16[1024,32]{0,1:T(8,128)(2,1)S(1)} %copy-done.23, ...), dimensions={1} | concatenate | bytes 12722176 | tf_op jit(solution)/shard_map/concatenate | solution.py:37
  512.8 9.1 %copy.254 = bf16[1024,3106]{1,0:T(8,128)(2,1)} copy(bf16[1024,3106]{0,1:T(8,128)(2,1)} %concatenate.100) | data formatting | bytes 12722176
  522.3 5.4 bitcast_convert_fusion.1
  527.7 7.5 %bitcast_convert_fusion = bf16[2,1024,1024]{1,2,0:T(8,128)(2,1)S(1)} fusion(bf16[16,2,64,1024]{3,2,1,0:T(8,128)(2,1)} %all-to-all-done, bf16[16,2,64,512]{3,2,0,1:T(8,128)(2,1)} %copy-done.31, bf16[16,2,64,512]{3,2,0,1:T(8,128)(2,1)S(1)} %copy-done.30), kind=kOutput, calls=%fused_computation.6 | convolution fusion | flops 4305453056 | bytes 12582912 | tf_op jit(solution)/shard_map/sjcf,sjcd->jfd/dot_general | solution.py:235
  538.6 16.6 %copy.256 = bf16[2,1024,1536]{2,0,1:T(2,128)(2,1)} copy(bf16[2,1024,1536]{1,2,0:T(8,128)(2,1)} %pad_maximum_fusion) | data formatting | bytes 12582912
  555.2 7.0 copy.270
  562.3 52.5 %reduce-scatter.12.cloned.1.call-done = bf16[64,3106]{1,0:T(8,128)(2,1)} async-done(((bf16[1024,3106]{1,0:T(8,128)(2,1)}), bf16[64,3106]{1,0:T(8,128)(2,1)}) %reduce-scatter.12.cloned.1.call-update) | async-done | bytes 397584
  616.4 4.8 all-to-all-start.9
  645.9 18.5 %all_to_all.57 = bf16[8,64,512]{2,1,0:T(8,128)(2,1)} all-to-all(bf16[8,64,512]{2,1,0:T(8,128)(2,1)S(1)} %broadcast_in_dim.107), channel_id=1, replica_groups=mesh['ctx'=8,'wsh'=16] {'ctx'}, dimensions={0} | all-to-all | bytes 1048576 | tf_op jit(solution)/shard_map/all_to_all | solution.py:49
  670.2 12.8 %all-to-all-done.6 = bf16[8,64,512]{2,1,0:T(8,128)(2,1)S(1)} async-done(((bf16[8,64,512]{2,1,0:T(8,128)(2,1)}), bf16[8,64,512]{2,1,0:T(8,128)(2,1)S(1)}, u32[]{:S(2)}, u32[]{:S(2)}) %all-to-all-start.6) | async-done | bytes 524320 | tf_op jit(solution)/shard_map/all_to_all | solution.py:49
  688.1 21.7 %all-to-all-done.8 = bf16[8,64,1024]{2,1,0:T(8,128)(2,1)S(1)} async-done(((bf16[8,64,1024]{2,1,0:T(8,128)(2,1)}), bf16[8,64,1024]{2,1,0:T(8,128)(2,1)S(1)}, u32[]{:S(2)}, u32[]{:S(2)}) %all-to-all-start.8) | async-done | bytes 1048608 | tf_op jit(solution)/shard_map/all_to_all | solution.py:49
  (224 shorter events, 169.3 us)
Async XLA Ops:
  7.2 256.8 %copy-start = (bf16[2,1024,512]{2,1,0:T(8,128)(2,1)S(1)}, bf16[2,1024,512]{2,1,0:T(8,128)(2,1)}, u32[]{:S(2)}) copy-start(bf16[2,1024,512]{2,1,0:T(8,128)(2,1)} %param.21) | copy-start | bytes 6291460
  7.2 72.3 %all-gather.3.cloned.1.call-start = ((), (), s32[]{:S(2)}) async-start(), calls=%async_computation.14 | async-start | bytes 6963200 | tf_op jit(solution)/shard_map/all_gather | solution.py:20
  11.6 73.1 %copy-start.3 = (bf16[1,128,1024]{2,1,0:T(8,128)(2,1)S(1)}, bf16[1,128,1024]{2,1,0:T(8,128)(2,1)}, u32[]{:S(2)}) copy-start(bf16[1,128,1024]{2,1,0:T(8,128)(2,1)} %param.12) | copy-start | bytes 786436
  11.6 112.6 %all-gather.5.cloned.1.call-start = ((), (), s32[]{:S(2)}) async-start(), calls=%async_computation.15 | async-start | bytes 2359296 | tf_op jit(solution)/shard_map/all_gather | solution.py:31
  13.8 73.2 %copy-start.24 = (s32[1,1,128,8]{2,3,1,0:T(8,128)S(1)}, s32[1,1,128,8]{2,3,1,0:T(8,128)}, u32[]{:S(2)}) copy-start(s32[1,1,128,8]{2,3,1,0:T(8,128)} %param.22) | copy-start | bytes 12292
  140.3 8.4 %copy-start.27 = (f32[128]{0:T(128)}, f32[128]{0:T(128)S(1)}, u32[]{:S(2)}) copy-start(f32[128]{0:T(128)S(1)} %add_rsqrt_fusion) | copy-start | bytes 1540
  140.4 8.2 %copy-start.8 = (bf16[128,1024]{1,0:T(8,128)(2,1)}, bf16[128,1024]{1,0:T(8,128)(2,1)S(1)}, u32[]{:S(2)}) copy-start(bf16[128,1024]{1,0:T(8,128)(2,1)S(1)} %multiply_convert_fusion.1) | copy-start | bytes 786436
  148.7 58.5 %all-to-all-start = ((bf16[16,2,64,1024]{3,2,1,0:T(8,128)(2,1)}), bf16[16,2,64,1024]{3,2,1,0:T(8,128)(2,1)}, u32[]{:S(2)}, u32[]{:S(2)}) async-start(bf16[16,2,64,1024]{3,2,1,0:T(8,128)(2,1)} %bitcast.339), calls=%async_computation | async-start | bytes 8388608 | tf_op jit(solution)/shard_map/all_to_all | solution.py:196
  207.1 56.8 %all-to-all-start.2 = ((bf16[16,2,64,1024]{3,2,1,0:T(8,128)(2,1)}), bf16[16,2,64,1024]{3,2,1,0:T(8,128)(2,1)}, u32[]{:S(2)}, u32[]{:S(2)}) async-start(bf16[16,2,64,1024]{3,2,1,0:T(8,128)(2,1)} %bitcast.340), calls=%async_computation.2 | async-start | bytes 8388608 | tf_op jit(solution)/shard_map/all_to_all | solution.py:221
  263.9 8.9 %copy-start.28 = (bf16[2,1024,1024]{2,1,0:T(8,128)(2,1)S(1)}, bf16[2,1024,1024]{2,1,0:T(8,128)(2,1)}, u32[]{:S(2)}) copy-start(bf16[2,1024,1024]{2,1,0:T(8,128)(2,1)} %param.20) | copy-start | bytes 12582916
  280.0 56.4 %all-to-all-start.3 = ((bf16[16,2,64,1024]{3,2,1,0:T(8,128)(2,1)}), bf16[16,2,64,1024]{3,2,1,0:T(8,128)(2,1)}, u32[]{:S(2)}, u32[]{:S(2)}) async-start(bf16[16,2,64,1024]{3,2,1,0:T(8,128)(2,1)} %copy.222), calls=%async_computation.3 | async-start | bytes 8388608 | tf_op jit(solution)/shard_map/all_to_all | solution.py:239
  291.1 50.1 %copy-start.15 = (f32[128,8]{1,0:T(8,128)S(1)}, f32[128,8]{1,0:T(8,128)}, u32[]{:S(2)}) copy-start(f32[128,8]{1,0:T(8,128)} %reshape.797) | copy-start | bytes 12292
  336.4 56.4 %all-to-all-start.1 = ((bf16[16,2,64,1024]{3,2,1,0:T(8,128)(2,1)}), bf16[16,2,64,1024]{3,2,1,0:T(8,128)(2,1)}, u32[]{:S(2)}, u32[]{:S(2)}) async-start(bf16[16,2,64,1024]{3,2,1,0:T(8,128)(2,1)} %copy.220), calls=%async_computation.1 | async-start | bytes 8388608 | tf_op jit(solution)/shard_map/all_to_all | solution.py:205
  340.9 136.8 %reduce-scatter.10.cloned.1.call-start = ((), (), s32[]{:S(2)}) async-start(), calls=%async_computation.16 | async-start | bytes 2359296
  392.8 7.7 %copy-start.14 = (f32[128,8]{1,0:T(8,128)S(1)}, f32[128,8]{1,0:T(8,128)}, u32[]{:S(2)}) copy-start(f32[128,8]{1,0:T(8,128)} %fusion.105) | copy-start | bytes 12292
  402.9 6.8 copy-start.13
  402.9 6.8 copy-start.26
  409.8 6.4 copy-start.5
  440.0 174.8 %reduce-scatter.12.cloned.1.call-start = ((), (), s32[]{:S(2)}) async-start(), calls=%async_computation.17 | async-start | bytes 6963200
  440.1 16.6 %copy-start.20 = (f32[128,64]{0,1:T(8,128)S(1)}, f32[128,64]{0,1:T(8,128)}, u32[]{:S(2)}) copy-start(f32[128,64]{0,1:T(8,128)} %copy-done.19) | copy-start | bytes 98308
  522.0 194.5 %reduce-scatter.14.cloned.1.call-start = ((), (), s32[]{:S(2)}) async-start(), calls=%async_computation.18 | async-start | bytes 7077888
  616.4 9.5 %all-to-all-start.9 = ((bf16[8,1,64]{2,1,0:T(2,128)(2,1)}), bf16[8,1,64]{2,1,0:T(2,128)(2,1)S(1)}, u32[]{:S(2)}, u32[]{:S(2)}) async-start(bf16[8,1,64]{2,1,0:T(2,128)(2,1)} %broadcast_in_dim.110), calls=%async_computation.9 | async-start | bytes 8192 | tf_op jit(solution)/shard_map/all_to_all | solution.py:49
  626.4 9.3 %all-to-all-start.4 = ((bf16[8,1,64]{2,1,0:T(2,128)(2,1)}), bf16[8,1,64]{2,1,0:T(2,128)(2,1)S(1)}, u32[]{:S(2)}, u32[]{:S(2)}) async-start(bf16[8,1,64]{2,1,0:T(2,128)(2,1)} %broadcast_in_dim.104), calls=%async_computation.4 | async-start | bytes 8192 | tf_op jit(solution)/shard_map/all_to_all | solution.py:49
  635.8 10.1 %all-to-all-start.10 = ((bf16[8,2,1024]{2,1,0:T(2,128)(2,1)}), bf16[8,2,1024]{2,1,0:T(2,128)(2,1)S(1)}, u32[]{:S(2)}, u32[]{:S(2)}) async-start(bf16[8,2,1024]{2,1,0:T(2,128)(2,1)} %reshape.837), calls=%async_computation.10 | async-start | bytes 65536 | tf_op jit(solution)/shard_map/all_to_all | solution.py:49
  665.2 50.3 %copy-start.22 = (f32[128,1024]{1,0:T(8,128)S(1)}, f32[128,1024]{1,0:T(8,128)}, u32[]{:S(2)}) copy-start(f32[128,1024]{1,0:T(8,128)} %get-tuple-element.168) | copy-start | bytes 1572868
  665.2 17.8 %all-to-all-start.6 = ((bf16[8,64,512]{2,1,0:T(8,128)(2,1)}), bf16[8,64,512]{2,1,0:T(8,128)(2,1)S(1)}, u32[]{:S(2)}, u32[]{:S(2)}) async-start(bf16[8,64,512]{2,1,0:T(8,128)(2,1)} %broadcast_in_dim.106), calls=%async_computation.6 | async-start | bytes 1048576 | tf_op jit(solution)/shard_map/all_to_all | solution.py:49
  683.1 33.4 %copy-start.11 = (bf16[8,64,512]{2,1,0:T(8,128)(2,1)}, bf16[8,64,512]{2,1,0:T(8,128)(2,1)S(1)}, u32[]{:S(2)}) copy-start(bf16[8,64,512]{2,1,0:T(8,128)(2,1)S(1)} %all-to-all-done.6) | copy-start | bytes 1572868
  684.2 25.6 %all-to-all-start.8 = ((bf16[8,64,1024]{2,1,0:T(8,128)(2,1)}), bf16[8,64,1024]{2,1,0:T(8,128)(2,1)S(1)}, u32[]{:S(2)}, u32[]{:S(2)}) async-start(bf16[8,64,1024]{2,1,0:T(8,128)(2,1)} %broadcast_in_dim.108), calls=%async_computation.8 | async-start | bytes 2097152 | tf_op jit(solution)/shard_map/all_to_all | solution.py:49
  709.8 6.7 copy-start.6
  711.1 24.8 %all-to-all-start.5 = ((bf16[8,64,1024]{2,1,0:T(8,128)(2,1)}), bf16[8,64,1024]{2,1,0:T(8,128)(2,1)}, u32[]{:S(2)}, u32[]{:S(2)}) async-start(bf16[8,64,1024]{2,1,0:T(8,128)(2,1)} %broadcast_in_dim.105), calls=%async_computation.5 | async-start | bytes 2097152 | tf_op jit(solution)/shard_map/all_to_all | solution.py:49
  716.5 18.4 %copy-start.7 = (bf16[8,64,1024]{2,1,0:T(8,128)(2,1)S(1)}, bf16[8,64,1024]{2,1,0:T(8,128)(2,1)}, u32[]{:S(2)}) copy-start(bf16[8,64,1024]{2,1,0:T(8,128)(2,1)} %copy-done.6) | copy-start | bytes 3145732
  720.9 17.0 %copy-start.1 = (bf16[2,1024,512]{2,1,0:T(8,128)(2,1)S(1)}, bf16[2,1024,512]{2,1,0:T(8,128)(2,1)}, u32[]{:S(2)}) copy-start(bf16[2,1024,512]{2,1,0:T(8,128)(2,1)} %param.21) | copy-start | bytes 6291460
  (15 other events, 49.2 us)
Sparse Core Ops, SparseCore 0:
  11.7 67.7 all-gather.2
  87.1 37.0 all-gather.4
  440.1 37.6 reduce-scatter.9
  522.1 92.6 reduce-scatter.11
  617.2 90.4 reduce-scatter.13
where the time goes:
time: 758 us; the launch traced here: 745 us
  waiting for transfers between devices  355 us (47%)
  local copies, waits for them, and re-layouts  140 us (18%)
  matrix products  117 us (15%)
  other arithmetic  51.6 us (7%)
  starting transfers between devices  47.8 us (6%)
  blocking collectives  18.5 us (2%)
  between operations  15.2 us (2%)
    unnamed x8, waiting for transfers between devices  65.8 us
    all_gather x1, waiting for transfers between devices, in_one_piece(): filled, at, done = (lax.all_gather(both, axis, axis=dim, tiled=True), 0, [])  65.7 us
    unnamed x82, local copies, waits for them, and re-layouts  51.2 us
    all_to_all x6, waiting for transfers between devices, from_everyone(): return lax.all_to_all(copies, axis, split_axis=0, concat_axis=0, tiled=True)  46.8 us
    all_to_all x1, waiting for transfers between devices, local(): lax.all_to_all(grad_copy, 'wsh', split_axis=0, concat_axis=0, tiled=True)  45.3 us
    all_to_all x1, waiting for transfers between devices, local(): lax.all_to_all(produced, 'wsh', split_axis=0, concat_axis=0, tiled=True)  40.9 us
    all_to_all x1, waiting for transfers between devices, local(): lax.all_to_all(grad_send, 'wsh', split_axis=0, concat_axis=0, tiled=True)  40.5 us
    all_to_all x1, waiting for transfers between devices, local(): lax.all_to_all(outgoing, 'wsh', split_axis=0, concat_axis=0, tiled=True)  28 us
  transfers between devices with their start and end apart: 15, of which 13 were waited for; matrix products, arithmetic and copies ran while one was open for 22% of the time, Pallas kernels for 0%

commit v1 on v0

v1 whole, which is shorter than its diff:
```python
import functools

import jax
import jax.numpy as jnp
from jax import lax
from jax.experimental import pallas as pl
from jax.experimental.pallas import tpu as pltpu
from jax.sharding import PartitionSpec as P

MESH = pl.DeviceIdType.MESH
F32 = jnp.float32
BF16 = jnp.bfloat16
DH = 64
EPS = 1e-05
ROPE_BASE = 10000.0
MASKED = -1e30
VMEM = pl.BlockSpec(memory_space=pltpu.VMEM)
NT = (((1,), (1,)), ((), ()))
TN = (((0,), (0,)), ((), ()))


def dot(a, b, dims=(((1,), (0,)), ((), ()))):
    return lax.dot_general(a, b, dims, preferred_element_type=F32)


def wsh_place():
    w = lax.axis_index("wsh")
    return w // 4, (w // 2) % 2, w % 2


def wsh_slot(a, b, core):
    return (a * 2 + b) * 2 + core


def wsh_device(a, b, core):
    return (lax.axis_index("ctx"), wsh_slot(a, b, core))


def ctx_place():
    c = lax.axis_index("ctx")
    return c % 4, c // 4


def ctx_slot(a, b):
    return b * 4 + a


def ctx_device(a, b):
    return (ctx_slot(a, b), lax.axis_index("wsh"))


def around(a, step):
    return lax.rem(a + step, 4)


def greet(peers):
    barrier = pltpu.get_barrier_semaphore()
    for peer in peers:
        pl.semaphore_signal(barrier, inc=1, device_id=peer, device_id_type=MESH)
    pl.semaphore_wait(barrier, len(peers))


def remote(src, dst, send, recv, k, device):
    return pltpu.make_async_remote_copy(
        src_ref=src,
        dst_ref=dst,
        send_sem=send.at[k],
        recv_sem=recv.at[k],
        device_id=device,
        device_id_type=MESH,
    )


def wsh_peers():
    a, b, core = wsh_place()
    return [
        wsh_device(around(a, 1), b, core),
        wsh_device(around(a, 3), b, core),
        wsh_device(around(a, 2), b, core),
        wsh_device(a, 1 - b, core),
        wsh_device(a, b, 1 - core),
    ]


def ctx_peers():
    a, b = ctx_place()
    return [
        ctx_device(around(a, 1), b),
        ctx_device(around(a, 3), b),
        ctx_device(around(a, 2), b),
        ctx_device(a, 1 - b),
    ]


def gather_steps(full, slot, device, a, b, send, recv, arrived):
    up, down, far = around(a, 1), around(a, 3), around(a, 2)
    other = 1 - b

    def push(k, sa, sb, to):
        at = full.at[slot(sa, sb)]
        copy = remote(at, at, send, recv, k, to)
        copy.start()
        return copy

    def landed(k, sa, sb):
        at = full.at[slot(sa, sb)]
        remote(at, at, send, recv, k, device(a, b)).wait_recv()
        arrived(k, sa, sb)

    sent = [
        push(3, a, b, device(a, other)),
        push(0, a, b, device(up, b)),
        push(1, a, b, device(down, b)),
        push(2, a, b, device(far, b)),
    ]
    landed(3, a, other)
    sent.append(push(4, a, other, device(up, b)))
    sent.append(push(5, a, other, device(down, b)))
    landed(0, down, b)
    landed(1, up, b)
    landed(2, far, b)
    sent.append(push(6, far, b, device(a, other)))
    landed(4, down, other)
    landed(5, up, other)
    landed(6, far, other)
    for copy in sent:
        copy.wait_send()


def gather_wsh(x, cid):
    rows, cols = x.shape

    def kernel(x_ref, full, send, recv, send_c, recv_c):
        a, b, core = wsh_place()
        greet(wsh_peers())
        full[wsh_slot(a, b, core)] = x_ref[...]
        slot = lambda sa, sb: wsh_slot(sa, sb, core)
        handed = []

        def hand(k, sa, sb):
            at = full.at[wsh_slot(sa, sb, core)]
            copy = remote(at, at, send_c, recv_c, k, wsh_device(a, b, 1 - core))
            copy.start()
            handed.append((copy, k, sa, sb))

        hand(7, a, b)
        gather_steps(full, slot, lambda sa, sb: wsh_device(sa, sb, core), a, b, send, recv, hand)
        for copy, k, sa, sb in handed:
            copy.wait_send()
            at = full.at[wsh_slot(sa, sb, 1 - core)]
            remote(at, at, send_c, recv_c, k, wsh_device(a, b, 1 - core)).wait_recv()

    return pl.pallas_call(
        kernel,
        out_shape=jax.ShapeDtypeStruct((16, rows, cols), x.dtype),
        in_specs=[VMEM],
        out_specs=VMEM,
        scratch_shapes=[pltpu.SemaphoreType.DMA((7,))] * 2 + [pltpu.SemaphoreType.DMA((8,))] * 2,
        compiler_params=pltpu.CompilerParams(
            collective_id=cid, has_side_effects=True, vmem_limit_bytes=32 << 20
        ),
        name="gather_wsh",
    )(x)


def gather_ctx(x, cid):
    rows, cols = x.shape

    def kernel(x_ref, full, send, recv):
        a, b = ctx_place()
        greet(ctx_peers())
        full[ctx_slot(a, b)] = x_ref[...]
        gather_steps(full, ctx_slot, ctx_device, a, b, send, recv, lambda *_: None)

    return pl.pallas_call(
        kernel,
        out_shape=jax.ShapeDtypeStruct((8, rows, cols), x.dtype),
        in_specs=[VMEM],
        out_specs=VMEM,
        scratch_shapes=[pltpu.SemaphoreType.DMA((7,))] * 2,
        compiler_params=pltpu.CompilerParams(
            collective_id=cid, has_side_effects=True, vmem_limit_bytes=32 << 20
        ),
        name="gather_ctx",
    )(x)


def scatter_steps(acc, land, slot, device, a, b, send, recv, ready, add):
    up, down, far = around(a, 1), around(a, 3), around(a, 2)
    other = 1 - b

    def push(k, sa, sb, to):
        copy = remote(acc.at[slot(sa, sb)], land.at[k], send, recv, k, to)
        copy.start()
        return copy

    def landed(k, sa, sb):
        remote(acc.at[slot(sa, sb)], land.at[k], send, recv, k, device(a, b)).wait_recv()
        add(sa, sb, k)

    sent = []
    ready(far, other)
    sent.append(push(0, far, other, device(a, other)))
    ready(up, other)
    sent.append(push(1, up, other, device(up, b)))
    ready(down, other)
    sent.append(push(2, down, other, device(down, b)))
    ready(up, b)
    sent.append(push(3, up, b, device(up, b)))
    ready(down, b)
    sent.append(push(4, down, b, device(down, b)))
    ready(far, b)
    landed(0, far, b)
    sent.append(push(5, far, b, device(far, b)))
    ready(a, other)
    landed(1, a, other)
    landed(2, a, other)
    sent.append(push(6, a, other, device(a, other)))
    ready(a, b)
    landed(3, a, b)
    landed(4, a, b)
    landed(5, a, b)
    landed(6, a, b)
    for copy in sent:
        copy.wait_send()


def wsh_sum_body(p_ref, acc, land, land_c, send, recv, send_c, recv_c):
    a, b, core = wsh_place()
    slot = lambda sa, sb: sa * 2 + sb
    far, up, down = around(a, 2), around(a, 1), around(a, 3)
    order = [(far, 1 - b), (up, 1 - b), (down, 1 - b), (up, b), (down, b), (far, b), (a, 1 - b), (a, b)]
    handed = []
    for k, (sa, sb) in enumerate(order):
        copy = remote(
            p_ref.at[slot(sa, sb), 1 - core],
            land_c.at[k],
            send_c,
            recv_c,
            k,
            wsh_device(a, b, 1 - core),
        )
        copy.start()
        handed.append(copy)
    count = [0]

    def ready(sa, sb):
        k = count[0]
        count[0] += 1
        handed[k].wait_recv()
        at = slot(sa, sb)
        acc[at] = (p_ref[at, core].astype(F32) + land_c[k].astype(F32)).astype(acc.dtype)

    def add(sa, sb, k):
        at = slot(sa, sb)
        acc[at] = (acc[at].astype(F32) + land[k].astype(F32)).astype(acc.dtype)

    scatter_steps(acc, land, slot, lambda sa, sb: wsh_device(sa, sb, core), a, b, send, recv, ready, add)
    for copy in handed:
        copy.wait_send()
    return slot(a, b)


def sum_wsh(p, cid):
    _, rows, cols = p.shape

    def kernel(p_ref, o_ref, acc, land, land_c, send, recv, send_c, recv_c):
        greet(wsh_peers())
        own = wsh_sum_body(p_ref, acc, land, land_c, send, recv, send_c, recv_c)
        o_ref[...] = acc[own]

    return pl.pallas_call(
        kernel,
        out_shape=jax.ShapeDtypeStruct((rows, cols), BF16),
        in_specs=[VMEM],
        out_specs=VMEM,
        scratch_shapes=[
            pltpu.VMEM((8, rows, cols), BF16),
            pltpu.VMEM((7, rows, cols), BF16),
            pltpu.VMEM((8, rows, cols), BF16),
        ]
        + [pltpu.SemaphoreType.DMA((7,))] * 2
        + [pltpu.SemaphoreType.DMA((8,))] * 2,
        compiler_params=pltpu.CompilerParams(
            collective_id=cid, has_side_effects=True, vmem_limit_bytes=48 << 20
        ),
        name="sum_wsh",
    )(p.reshape(8, 2, rows, cols))


def sum_ctx(p, cid):
    _, rows, cols = p.shape

    def kernel(p_ref, o_ref, acc, land, send, recv):
        a, b = ctx_place()
        greet(ctx_peers())

        def ready(sa, sb):
            at = ctx_slot(sa, sb)
            acc[at] = p_ref[at]

        def add(sa, sb, k):
            at = ctx_slot(sa, sb)
            acc[at] = (acc[at].astype(F32) + land[k].astype(F32)).astype(acc.dtype)

        scatter_steps(acc, land, ctx_slot, ctx_device, a, b, send, recv, ready, add)
        o_ref[...] = acc[ctx_slot(a, b)]

    return pl.pallas_call(
        kernel,
        out_shape=jax.ShapeDtypeStruct((rows, cols), p.dtype),
        in_specs=[VMEM],
        out_specs=VMEM,
        scratch_shapes=[
            pltpu.VMEM((8, rows, cols), p.dtype),
            pltpu.VMEM((7, rows, cols), p.dtype),
        ]
        + [pltpu.SemaphoreType.DMA((7,))] * 2,
        compiler_params=pltpu.CompilerParams(
            collective_id=cid, has_side_effects=True, vmem_limit_bytes=32 << 20
        ),
        name="sum_ctx",
    )(p)


def sum_all(p, cid):
    _, rows, cols = p.shape
    part = rows // 8

    def kernel(p_ref, o_ref, acc, land, land_c, acc2, land2, *sems):
        send, recv, send_c, recv_c, send2, recv2, send3, recv3 = sems
        greet(wsh_peers() + ctx_peers())
        own = wsh_sum_body(p_ref, acc, land, land_c, send, recv, send_c, recv_c)
        a, b = ctx_place()
        acc2[...] = acc[own].astype(F32).reshape(8, part, cols)

        def add(sa, sb, k):
            acc2[ctx_slot(sa, sb)] += land2[k]

        scatter_steps(
            acc2, land2, ctx_slot, ctx_device, a, b, send2, recv2, lambda *_: None, add
        )
        o_ref[ctx_slot(a, b)] = acc2[ctx_slot(a, b)]
        gather_steps(o_ref, ctx_slot, ctx_device, a, b, send3, recv3, lambda *_: None)

    out = pl.pallas_call(
        kernel,
        out_shape=jax.ShapeDtypeStruct((8, part, cols), F32),
        in_specs=[VMEM],
        out_specs=VMEM,
        scratch_shapes=[
            pltpu.VMEM((8, rows, cols), BF16),
            pltpu.VMEM((7, rows, cols), BF16),
            pltpu.VMEM((8, rows, cols), BF16),
            pltpu.VMEM((8, part, cols), F32),
            pltpu.VMEM((7, part, cols), F32),
        ]
        + [pltpu.SemaphoreType.DMA((7,))] * 2
        + [pltpu.SemaphoreType.DMA((8,))] * 2
        + [pltpu.SemaphoreType.DMA((7,))] * 4,
        compiler_params=pltpu.CompilerParams(
            collective_id=cid, has_side_effects=True, vmem_limit_bytes=48 << 20
        ),
        name="sum_all",
    )(p.reshape(8, 2, rows, cols))
    return out.reshape(rows, cols)


def compute(kernel, outs, scratch=(), limit=48, name=None):
    return pl.pallas_call(
        kernel,
        out_shape=[jax.ShapeDtypeStruct(s, d) for s, d in outs],
        scratch_shapes=list(scratch),
        compiler_params=pltpu.CompilerParams(vmem_limit_bytes=limit << 20),
        name=name,
    )


def rms_scale(x):
    return lax.rsqrt(jnp.mean(x * x, -1, keepdims=True) + EPS)


def norm_back(u, x, scale):
    return scale * u - x * scale * scale * scale * jnp.mean(u * x, -1, keepdims=True)


def low_half(shape):
    return lax.broadcasted_iota(jnp.int32, shape, len(shape) - 1) % DH < DH // 2


def rotate(v, cos, sin):
    width = v.shape[-1]
    turned = jnp.where(
        low_half(v.shape), -pltpu.roll(v, width - DH // 2, 1), pltpu.roll(v, DH // 2, 1)
    )
    return v * cos + turned * sin


def unrotate(v, cos, sin):
    width = v.shape[-1]
    scaled = v * sin
    turned = jnp.where(
        low_half(v.shape), pltpu.roll(scaled, width - DH // 2, 1), -pltpu.roll(scaled, DH // 2, 1)
    )
    return v * cos + turned


def project_kernel(tok, w, cos, sin, normed_o, q_o, kv_o, misc_o):
    x = tok[...].astype(F32)
    misc = w[:, 2048:2176].astype(F32).T
    misc_o[...] = misc
    normed = (x * rms_scale(x) * misc[96:97]).astype(BF16)
    normed_o[...] = normed
    c, s = cos[...], sin[...]
    q = dot(normed, w[:, :1024])
    q_o[...] = rotate(q, c, s).astype(BF16)
    k = dot(normed, w[:, 1024:1536])
    kv_o[:, :512] = rotate(k, c[:, :512], s[:, :512]).astype(BF16)
    kv_o[:, 512:] = dot(normed, w[:, 1536:2048]).astype(BF16)


def two_heads(ref, g):
    return jnp.concatenate(
        [ref[:, g * 128 : g * 128 + 64], ref[:, g * 128 + 64 : g * 128 + 128]], 0
    )


def side_by_side(rows):
    return jnp.concatenate([rows[:128], rows[128:]], 1)


def visible_mask():
    row = lax.broadcasted_iota(jnp.int32, (256, 1024), 0) % 128
    col = lax.broadcasted_iota(jnp.int32, (256, 1024), 1)
    return col <= row + lax.axis_index("ctx") * 128


def attend_kernel(q, kv, tok, wo, misc, merged_o, mid_o, normed_o, lse_o):
    visible = visible_mask()
    for g in range(8):
        keys = kv[:, g * 64 : g * 64 + 64]
        values = kv[:, 512 + g * 64 : 512 + g * 64 + 64]
        scores = jnp.where(visible, dot(two_heads(q, g), keys, NT) * DH**-0.5, MASKED)
        top = jnp.max(scores, -1, keepdims=True)
        raised = jnp.exp(scores - top)
        total = jnp.sum(raised, -1, keepdims=True)
        lse_o[g] = top + jnp.log(total)
        probs = (raised * (1.0 / total)).astype(BF16)
        merged_o[:, g * 128 : g * 128 + 128] = side_by_side(dot(probs, values)).astype(BF16)
    mid = tok[...].astype(F32) + dot(merged_o[...], wo[...])
    mid_o[...] = mid
    normed_o[...] = (mid * rms_scale(mid) * misc[97:98, :]).astype(BF16)


def parts_of(v):
    high = v.astype(BF16)
    rest = v - high.astype(F32)
    middle = rest.astype(BF16)
    return high, middle, (rest - middle.astype(F32)).astype(BF16)


def experts_kernel(
    x, g, w_in, w_out, misc, mask, pay, wg, sel, buf, gbuf, gcol, ggcol, gp, hidden, gact, gcopy
):
    own = lax.axis_index("wsh") * 2
    tri = (
        lax.broadcasted_iota(jnp.int32, (128, 128), 0)
        < lax.broadcasted_iota(jnp.int32, (128, 128), 1)
    ).astype(BF16)
    router = misc[0:32, :].astype(BF16)
    experts = lax.broadcasted_iota(jnp.int32, (32, 128), 0)
    slots = lax.broadcasted_iota(jnp.int32, (64, 128), 0).astype(F32)

    def pick(s, _):
        rows = pl.ds(pl.multiple_of(s * 128, 128), 128)
        chosen = mask[s]
        logits = jnp.where(chosen > 0, dot(router, x[rows, :], NT), MASKED)
        raised = jnp.exp(logits - jnp.max(logits, 0, keepdims=True)) * chosen
        gates = raised / jnp.sum(raised, 0, keepdims=True)
        earlier = dot(chosen.astype(BF16), tri)
        place, gate = [], []
        for j in range(2):
            is_own = experts == own + j
            row = lambda v: jnp.sum(jnp.where(is_own, v, 0.0), 0, keepdims=True)
            hit = (slots == row(earlier)) & (row(chosen) > 0)
            place.append(hit.astype(F32))
            gate.append(jnp.sum(jnp.where(hit, row(gates), 0.0), 1, keepdims=True))
        both = jnp.concatenate(place, 0).astype(BF16)
        sel[s] = both
        xb = dot(both, x[rows, :]).astype(BF16)
        gb = dot(both, g[rows, :]).astype(BF16)
        at = pl.ds(pl.multiple_of(s * 64, 64), 64)
        for j in range(2):
            buf[j, at, :] = xb[j * 64 : j * 64 + 64]
            gbuf[j, at, :] = gb[j * 64 : j * 64 + 64]
            gcol[j, at, :] = gate[j]
        return _

    lax.fori_loop(0, 16, pick, 0)

    def tile(i, _):
        j = i // 4
        at = pl.ds(pl.multiple_of((i % 4) * 256, 256), 256)
        act = dot(buf[j, at, :], w_in[j], NT)
        gate, up = act[:, :512], act[:, 512:]
        s = jax.nn.sigmoid(gate)
        h = (gate * s * up).astype(BF16)
        hidden[j, at, :] = h
        produced = dot(h, w_out[j], NT).astype(BF16).astype(F32)
        gate_col = gcol[j, at, :]
        gr = gbuf[j, at, :].astype(F32)
        ggcol[j, at, :] = jnp.sum(gr * produced, 1, keepdims=True)
        gbuf[j, at, :] = (produced * gate_col).astype(BF16)
        gpt = (gr * gate_col).astype(BF16)
        gp[j, at, :] = gpt
        gh = dot(gpt, w_out[j])
        ga_gate = (gh * up * s * (1.0 + gate * (1.0 - s))).astype(BF16)
        ga_up = (gh * gate * s).astype(BF16)
        ga = jnp.concatenate([ga_gate, ga_up], 1)
        gact[j, at, :] = ga
        gcopy[j, at, :] = dot(ga, w_in[j]).astype(BF16)
        return _

    lax.fori_loop(0, 8, tile, 0)

    def weights(i, _):
        j = i // 4
        at = pl.ds(pl.multiple_of((i % 4) * 256, 256), 256)
        gi = dot(gact[j, :, at], buf[j], TN).astype(BF16)
        go = dot(gp[j, :, at], hidden[j], TN).astype(BF16)
        c = (i % 4) * 2
        for h in range(2):
            wg[c + h, j, :, :1024] = gi[h * 128 : h * 128 + 128]
            wg[c + h, j, :, 1024:] = go[h * 128 : h * 128 + 128]
        return _

    lax.fori_loop(0, 8, weights, 0)
    lane = lax.broadcasted_iota(jnp.int32, (64, 128), 1)

    def combine(s, _):
        at = pl.ds(pl.multiple_of(s * 64, 64), 64)
        both = sel[s]
        rows = lambda ref: jnp.concatenate([ref[0, at, :], ref[1, at, :]], 0)
        pay[s, :, :1024] = dot(both, rows(gbuf), TN).astype(BF16)
        pay[s, :, 1024:2048] = dot(both, rows(gcopy), TN).astype(BF16)
        cells = []
        for j in range(2):
            parts = parts_of(ggcol[j, at, :])
            cell = jnp.zeros((64, 128), F32)
            for n, part in enumerate(parts):
                cell = jnp.where(lane == own + j + 32 * n, part.astype(F32), cell)
            cells.append(cell.astype(BF16))
        pay[s, :, 2048:] = dot(both, jnp.concatenate(cells, 0), TN).astype(BF16)
        return _

    lax.fori_loop(0, 16, combine, 0)


def split_dot(a, b, dims):
    high = a.astype(BF16)
    rest = (a - high.astype(F32)).astype(BF16)
    return dot(high, b, dims) + dot(rest, b, dims)


def back_kernel(
    back, mid_r, cot, misc, mask, normed, merged, q, kv, lse, wo, cos, sin,
    out_o, gmid_o, gkv_o, gq_o, gwo_o, gmisc_o, gm, dkv,
):
    mid = mid_r[...]
    out_o[...] = (mid + back[:, :1024].astype(F32)).astype(BF16)
    cells = back[:, 2048:].astype(F32)
    ggates = cells[:, :32] + cells[:, 32:64] + cells[:, 64:96]
    router = misc[0:32, :].astype(BF16)
    chosen = mask[...]
    logits = jnp.where(chosen > 0, dot(normed[...], router, NT), MASKED)
    raised = jnp.exp(logits - jnp.max(logits, 1, keepdims=True)) * chosen
    gates = raised / jnp.sum(raised, 1, keepdims=True)
    glogits = gates * (ggates - jnp.sum(gates * ggates, 1, keepdims=True))
    scale = rms_scale(mid)
    gnormed = back[:, 1024:2048].astype(F32) + split_dot(glogits, router, (((1,), (0,)), ((), ())))
    gmisc_o[0:32, :] = split_dot(glogits, normed[...], TN)
    gmisc_o[32:33, :] = jnp.sum(gnormed * mid * scale, 0, keepdims=True)
    gmid = cot[...].astype(F32) + norm_back(gnormed * misc[97:98, :], mid, scale)
    gmid_o[...] = gmid
    branch = gmid.astype(BF16)
    gwo_o[...] = dot(merged[...], branch, TN).astype(BF16)
    gm[...] = dot(branch, wo[...], NT).astype(BF16)
    visible = visible_mask()
    gq = []
    for g in range(8):
        keys = kv[:, g * 64 : g * 64 + 64]
        values = kv[:, 512 + g * 64 : 512 + g * 64 + 64]
        queries, grads = two_heads(q, g), two_heads(gm, g)
        scores = jnp.where(visible, dot(queries, keys, NT) * DH**-0.5, MASKED)
        probs = jnp.exp(scores - lse[g])
        gprobs = dot(grads, values, NT)
        inner = jnp.sum(probs * gprobs, -1, keepdims=True)
        graw = (probs * (gprobs - inner) * DH**-0.5).astype(BF16)
        gq.append(side_by_side(dot(graw, keys)))
        dkv[g * 64 : g * 64 + 64, :] = dot(queries, graw, TN)
        dkv[512 + g * 64 : 512 + g * 64 + 64, :] = dot(grads, probs.astype(BF16), TN)
    gq_o[...] = unrotate(jnp.concatenate(gq, 1), cos[...], sin[...]).astype(BF16)
    for c in range(8):
        gkv_o[c] = dkv[:, c * 128 : c * 128 + 128].T.astype(BF16)


def finish_kernel(gkv, gq, normed, w, tok, gmid, cos, sin, misc, gwo, gmisc, tgrad_o, pack_o, gall):
    c, s = cos[:, :512], sin[:, :512]
    gall[:, :1024] = gq[...]
    gall[:, 1024:1536] = unrotate(gkv[:, :512].astype(F32), c, s).astype(BF16)
    gall[:, 1536:] = gkv[:, 512:]
    x = tok[...].astype(F32)
    scale = rms_scale(x)
    gnormed = dot(gall[...], w[:, :2048], NT)
    pack_o[:, :2048] = dot(normed[...], gall[...], TN).astype(BF16)
    pack_o[:, 2048:3072] = gwo[...]
    gain = jnp.sum(gnormed * x * scale, 0, keepdims=True)
    rows = jnp.concatenate([gmisc[0:33, :], gain, jnp.zeros((94, 1024), F32)], 0)
    pack_o[:, 3072:] = rows.T.astype(BF16)
    tgrad_o[...] = (gmid[...] + norm_back(gnormed * misc[96:97, :], x, scale)).astype(BF16)


def local(
    tokens, gain_attn, w_query, w_key, w_value, w_output, gain_moe, w_router, w_in, w_out, routes,
    cotangent,
):
    tok = tokens.reshape(128, 1024)
    cot = cotangent.reshape(128, 1024)
    chosen = routes.reshape(128, 8)
    own_mask = jnp.sum(
        (chosen[:, :, None] == jnp.arange(32, dtype=jnp.int32)).astype(F32), 1
    )
    low_mask = own_mask.astype(BF16)
    pack = jnp.concatenate(
        [
            w_query, w_key, w_value, w_router, low_mask[:64], low_mask[64:],
            gain_attn[:, None], gain_moe[:, None], jnp.zeros((64, 30), BF16),
        ],
        1,
    )
    wo = lax.all_gather(w_output, "wsh", axis=0, tiled=True)
    cot_all = lax.all_gather(cot, "wsh", axis=0, tiled=True)
    positions = (lax.axis_index("ctx") * 128 + jnp.arange(128, dtype=jnp.int32)).astype(F32)
    frequencies = ROPE_BASE ** (-jnp.arange(DH // 2, dtype=F32) * 2.0 / DH)
    angles = positions[:, None] * frequencies[None, :]
    cos = jnp.tile(jnp.cos(angles), (1, 32))
    sin = jnp.tile(jnp.sin(angles), (1, 32))

    w = gather_wsh(pack, 0).reshape(1024, 2176)
    t, d = 128, 1024
    normed, q, kv, misc = compute(
        project_kernel,
        [((t, d), BF16), ((t, d), BF16), ((t, d), BF16), ((128, d), F32)],
        name="project",
    )(tok, w, cos, sin)
    kv_all = gather_ctx(kv, 1).reshape(1024, 1024)
    merged, mid, normed_moe, lse = compute(
        attend_kernel,
        [((t, d), BF16), ((t, d), F32), ((t, d), BF16), ((8, 256, 1), F32)],
        name="attend",
    )(q, kv_all, tok, wo, misc)
    x_all = gather_wsh(normed_moe, 2).reshape(2048, 1024)
    mask = misc[32:96].reshape(2, 32, 16, 64).transpose(2, 1, 0, 3).reshape(16, 32, 128)
    e = 1024
    pay, wg = compute(
        experts_kernel,
        [((16, t, 2176), BF16), ((8, 2, 128, 1536), BF16)],
        [
            pltpu.VMEM((16, 128, 128), BF16),
            pltpu.VMEM((2, e, d), BF16),
            pltpu.VMEM((2, e, d), BF16),
            pltpu.VMEM((2, e, 1), F32),
            pltpu.VMEM((2, e, 1), F32),
            pltpu.VMEM((2, e, d), BF16),
            pltpu.VMEM((2, e, 512), BF16),
            pltpu.VMEM((2, e, d), BF16),
            pltpu.VMEM((2, e, d), BF16),
        ],
        limit=62,
        name="experts",
    )(x_all, cot_all, w_in, w_out, misc, mask)
    expert_grads = lax.psum_scatter(wg, "ctx", scatter_dimension=0, tiled=False).astype(F32)
    back = sum_wsh(pay, 3)
    output, gmid, gkv, gq, gwo, gmisc = compute(
        back_kernel,
        [
            ((t, d), BF16), ((t, d), F32), ((8, t, d), BF16), ((t, d), BF16), ((d, d), BF16),
            ((40, d), F32),
        ],
        [pltpu.VMEM((t, d), BF16), pltpu.VMEM((d, d), F32)],
        name="back",
    )(back, mid, cot, misc, own_mask, normed_moe, merged, q, kv_all, lse, wo, cos, sin)
    gkv_own = sum_ctx(gkv, 4)
    tokens_grad, packed = compute(
        finish_kernel,
        [((t, d), BF16), ((d, 3200), BF16)],
        [pltpu.VMEM((t, 2048), BF16)],
        name="finish",
    )(gkv_own, gq, normed, w, tok, gmid, cos, sin, misc, gwo, gmisc)
    sums = sum_all(packed.reshape(16, 64, 3200), 5)
    return (
        output.reshape(1, 128, 1024),
        tokens_grad.reshape(1, 128, 1024),
        sums[:, 3105],
        sums[:, :1024],
        sums[:, 1024:1536],
        sums[:, 1536:2048],
        sums[:, 2048:3072],
        sums[:, 3104],
        sums[:, 3072:3104],
        expert_grads[:, :, :1024],
        expert_grads[:, :, 1024:],
    )


def solution(mesh):
    return jax.shard_map(
        local,
        mesh=mesh,
        in_specs=(
            P("wsh", "ctx", None),
            P("wsh"),
            P("wsh", None),
            P("wsh", None),
            P("wsh", None),
            P("wsh", None),
            P("wsh"),
            P("wsh", None),
            P("wsh", None, None),
            P("wsh", None, None),
            P("wsh", "ctx", None, None),
            P("wsh", "ctx", None),
        ),
        out_specs=(
            P("wsh", "ctx", None),
            P("wsh", "ctx", None),
            P("wsh"),
            P("wsh", None),
            P("wsh", None),
            P("wsh", None),
            P("wsh", None),
            P("wsh"),
            P("wsh", None),
            P("wsh", "ctx", None),
            P("wsh", "ctx", None),
        ),
        check_vma=False,
    )
```

time: 758 us -> 388 us (0.51); the launches traced: 745 us -> 386 us
  waiting for transfers between devices: 355 us -> 5.13 us
  Pallas kernels: 0 us -> 339 us
  matrix products: 117 us -> 0 us
  local copies, waits for them, and re-layouts: 140 us -> 25.3 us
  other arithmetic: 51.6 us -> 2.18 us
  starting transfers between devices: 47.8 us -> 0.11 us
  blocking collectives: 18.5 us -> 0 us
    pallas_call x0 -> x11, Pallas kernels: none -> 339 us  [the longest x1 68.3 us: sum_ctx(): pl.pallas_call(kernel, out_shape=jax.ShapeDtypeStruct((rows, cols), p.dty...]
    all_to_all x10 -> x0, waiting for transfers between devices: 202 us -> none  [the longest x6 46.8 us: from_everyone(): return lax.all_to_all(copies, axis, split_axis=0, concat_axis=0, tiled=True)]
    dot_general x27 -> x0, matrix products: 117 us -> none  [the longest x1 16.5 us: backward_one(): jnp.einsum('grtj,jgd->tgrd', grad_raw, key_seq, preferred_element_type=jn...]
    all_gather x2, waiting for transfers between devices: 87.9 us -> 3.74 us  [the longest x1 3.72 us: local(): cot_all = lax.all_gather(cot, 'wsh', axis=0, tiled=True)]
    unnamed x8 -> x3, waiting for transfers between devices: 65.8 us -> 1.39 us
    all_to_all x10 -> x0, starting transfers between devices: 47.2 us -> none  [the longest x6 26.6 us: from_everyone(): return lax.all_to_all(copies, axis, split_axis=0, concat_axis=0, tiled=True)]
    unnamed x82 -> x54, local copies, waits for them, and re-layouts: 51.2 us -> 16.2 us
    concatenate x3 -> x1, local copies, waits for them, and re-layouts: 29.1 us -> 1.22 us  [local(): jnp.concatenate([w_query, w_key, w_value, w_router, low_mask[:64], low_ma...]
  transfers between devices with their start and end apart: 15 -> 3, of which waited for: 13 -> 1; matrix products, arithmetic and copies ran while one was open for 22% -> 2% of each run, Pallas kernels for 0% -> 75%
where the time goes in v1:
time: 388 us; the launch traced here: 386 us
  Pallas kernels  339 us (87%)
  local copies, waits for them, and re-layouts  25.3 us (7%)
  between operations  14.2 us (4%)
  waiting for transfers between devices  5.13 us (1%)
    pallas_call x1, Pallas kernels, sum_ctx(): pl.pallas_call(kernel, out_shape=jax.ShapeDtypeStruct((rows, cols), p.dty...  68.3 us
    pallas_call x2, Pallas kernels, gather_wsh(): pl.pallas_call(kernel, out_shape=jax.ShapeDtypeStruct((16, rows, cols), x...  60.9 us
    pallas_call x1, Pallas kernels, sum_all(): pl.pallas_call(kernel, out_shape=jax.ShapeDtypeStruct((8, part, cols), F3...  56.4 us
    pallas_call x1, Pallas kernels, local(): compute(experts_kernel, [((16, t, 2176), BF16), ((8, 2, 128, 1536), BF16)...  49.7 us
    pallas_call x1, Pallas kernels, sum_wsh(): pl.pallas_call(kernel, out_shape=jax.ShapeDtypeStruct((rows, cols), BF16)...  47.4 us
    pallas_call x1, Pallas kernels, gather_ctx(): pl.pallas_call(kernel, out_shape=jax.ShapeDtypeStruct((8, rows, cols), x....  22.6 us
    unnamed x54, local copies, waits for them, and re-layouts  16.2 us
    pallas_call x1, Pallas kernels, local(): compute(back_kernel, [((t, d), BF16), ((t, d), F32), ((8, t, d), BF16), (...  15 us
  transfers between devices with their start and end apart: 3, of which 1 were waited for; matrix products, arithmetic and copies ran while one was open for 2% of the time, Pallas kernels for 75%

profile of v1, /device:TPU:2, one launch (start us, length us, event | category | flops | bytes accessed | tf_op | source)
XLA Modules:
  0.0 386.2 jit_solution(5463600494407972167)
XLA Ops:
  8.7 0.8 copy.43
  9.5 0.8 copy.44
  10.2 0.8 copy.42
  11.0 0.7 convert_reduce_fusion
  12.6 1.2 concatenate.3.x_ref
  13.8 30.1 %gather_wsh.2 = bf16[16,64,2176]{2,1,0:T(8,128)(2,1)S(1)} custom-call(bf16[64,2176]{1,0:T(8,128)(2,1)S(1)} %concatenate.3.x_ref), custom_call_target="tpu_custom_call" | custom-call | tf_op jit(solution)/shard_map/gather_wsh/pallas_call | solution.py:153
  43.9 2.0 copy-done
  45.9 3.4 project.1
  50.8 0.7 copy-done.24
  52.0 1.0 reshape.134.mask
  53.0 0.9 copy-done.25
  54.0 22.6 %gather_ctx.1 = bf16[8,128,1024]{2,1,0:T(8,128)(2,1)S(1)} custom-call(bf16[128,1024]{1,0:T(8,128)(2,1)S(1)} %copy-done.25), custom_call_target="tpu_custom_call" | custom-call | tf_op jit(solution)/shard_map/gather_ctx/pallas_call | solution.py:175
  76.7 1.1 copy-done.13
  77.8 7.7 %attend.1 = (bf16[128,1024]{1,0:T(8,128)(2,1)S(1)}, f32[128,1024]{1,0:T(8,128)S(1)}, bf16[128,1024]{1,0:T(8,128)(2,1)S(1)}, f32[8,256,1]{2,1,0:T(8,128)S(1)}) custom-call(bf16[128,1024]{1,0:T(8,128)(2,1)S(1)} %copy-done.13, bf16[1024,1024]{1,0:T(8,128)(2,1)S(1)} %bitcast.24, bf16[128,1024]{1,0:T(8,128)(2,1)S(1)} %bitcast.32, ...), custom_call_target="tpu_custom_call" | custom-call | tf_op jit(solution)/shard_map/attend/pallas_call | solution.py:657
  85.5 1.0 copy-done.10
  86.5 0.8 copy-done.18
  88.0 30.9 %gather_wsh.3 = bf16[16,128,1024]{2,1,0:T(8,128)(2,1)S(1)} custom-call(bf16[128,1024]{1,0:T(8,128)(2,1)S(1)} %get-tuple-element.32.x_ref.normed), custom_call_target="tpu_custom_call" | custom-call | tf_op jit(solution)/shard_map/gather_wsh/pallas_call | solution.py:153
  118.9 2.1 copy-done.2
  121.7 3.7 all-gather.6.cloned.1.call-done
  125.4 49.7 %experts.1 = (bf16[16,128,2176]{2,1,0:T(8,128)(2,1)}, bf16[8,2,128,1536]{3,2,1,0:T(8,128)(2,1)}) custom-call(bf16[2048,1024]{1,0:T(8,128)(2,1)} %bitcast.26, bf16[2048,1024]{1,0:T(8,128)(2,1)} %bitcast.37, bf16[2,1024,1024]{2,1,0:T(8,128)(2,1)} %w_in.1, bf16[2,1024,512]{2,1,0:T(8,128)(2,1)} %w_out.1, f32[128,1024]{1,0:T(8,128)} %copy-done.3, ...), custom_call_target="tpu_custom_call" | custom-call | tf_op jit(solution)/shard_map/experts/pallas_call | solution.py:665
  175.2 47.4 %sum_wsh.1.back = bf16[128,2176]{1,0:T(8,128)(2,1)S(1)} custom-call(bf16[8,2,128,2176]{3,2,1,0:T(8,128)(2,1)} %bitcast.35), custom_call_target="tpu_custom_call" | custom-call | tf_op jit(solution)/shard_map/sum_wsh/pallas_call | solution.py:272
  222.7 15.0 %back.1 = (bf16[128,1024]{1,0:T(8,128)(2,1)}, f32[128,1024]{1,0:T(8,128)S(1)}, bf16[8,128,1024]{2,1,0:T(8,128)(2,1)}, bf16[128,1024]{1,0:T(8,128)(2,1)S(1)}, bf1...) custom-call(bf16[128,2176]{1,0:T(8,128)(2,1)S(1)} %sum_wsh.1.back, f32[128,1024]{1,0:T(8,128)S(1)} %copy-done.19, ...), custom_call_target="tpu_custom_call" | custom-call | tf_op jit(solution)/shard_map/back/pallas_call | solution.py:684
  237.8 1.6 copy-done.9
  239.4 68.3 %sum_ctx.1.gkv = bf16[128,1024]{1,0:T(8,128)(2,1)S(1)} custom-call(bf16[8,128,1024]{2,1,0:T(8,128)(2,1)S(1)} %copy-done.9), custom_call_target="tpu_custom_call" | custom-call | tf_op jit(solution)/shard_map/sum_ctx/pallas_call | solution.py:309
  307.7 1.6 copy-done.8
  309.3 7.8 %finish.1 = (bf16[128,1024]{1,0:T(8,128)(2,1)}, bf16[1024,3200]{1,0:T(8,128)(2,1)}) custom-call(bf16[128,1024]{1,0:T(8,128)(2,1)S(1)} %sum_ctx.1.gkv, bf16[128,1024]{1,0:T(8,128)(2,1)S(1)} %get-tuple-element.39.gq, bf16[128,1024]{1,0:T(8,128)(2,1)S(1)} %copy-done.21, bf16[1024,2176]{1,0:T(8,128)(2,1)} %bitcast.23, bf16[128,1024]{1,0:T(8,128)(2,1)S(1)} %bitcast.33, ...), custom_call_target="tpu_custom_call" | custom-call | tf_op jit(solution)/shard_map/finish/pallas_call | solution.py:694
  317.1 56.4 %sum_all.1 = f32[8,8,3200]{2,1,0:T(8,128)S(1)} custom-call(bf16[8,2,64,3200]{3,2,1,0:T(8,128)(2,1)} %bitcast.36), custom_call_target="tpu_custom_call" | custom-call | tf_op jit(solution)/shard_map/sum_all/pallas_call | solution.py:346
  374.9 0.7 fusion.1
  375.6 0.8 fusion
  376.5 1.3 bitcast_convert_fusion
  377.8 0.8 slice.58
  378.6 1.1 slice.57
  (68 shorter events, 7.1 us)
Async XLA Ops:
  7.2 69.5 %all-gather.4.cloned.1.call-start = ((), (), s32[]{:S(2)}) async-start(), calls=%async_computation.1 | async-start | bytes 2228224 | tf_op jit(solution)/shard_map/all_gather | solution.py:641
  7.9 117.5 %all-gather.6.cloned.1.call-start = ((), (), s32[]{:S(2)}) async-start(), calls=%async_computation.3 | async-start | bytes 4456448 | tf_op jit(solution)/shard_map/all_gather | solution.py:642
  8.7 367.8 %reduce-scatter.2.cloned.1.call-start = ((), (), s32[]{:S(2)}) async-start(), calls=%async_computation.2 | async-start | bytes 7077888 | tf_op jit(solution)/shard_map/reduce_scatter | solution.py:682
  12.0 33.9 %copy-start.7 = (bf16[1,128,1024]{2,1,0:T(8,128)(2,1)S(1)}, bf16[1,128,1024]{2,1,0:T(8,128)(2,1)}, u32[]{:S(2)}) copy-start(bf16[1,128,1024]{2,1,0:T(8,128)(2,1)} %param.12) | copy-start | bytes 786436
  12.6 36.8 %copy-start.5 = (f32[128,1024]{1,0:T(8,128)}, f32[128,1024]{1,0:T(8,128)S(1)}, u32[]{:S(2)}) copy-start(f32[128,1024]{1,0:T(8,128)S(1)} %copy.45.cos) | copy-start | bytes 1572868
  43.9 2.0 copy-start
  49.3 0.7 copy-start.12
  50.1 0.7 copy-start.20
  50.8 0.7 copy-start.24
  51.5 34.1 %copy-start.3 = (f32[128,1024]{1,0:T(8,128)}, f32[128,1024]{1,0:T(8,128)S(1)}, u32[]{:S(2)}) copy-start(f32[128,1024]{1,0:T(8,128)S(1)} %get-tuple-element.31.misc) | copy-start | bytes 1572868
  53.0 0.9 copy-start.25
  76.6 42.3 %copy-start.1 = (bf16[8,128,1024]{2,1,0:T(8,128)(2,1)}, bf16[8,128,1024]{2,1,0:T(8,128)(2,1)S(1)}, u32[]{:S(2)}) copy-start(bf16[8,128,1024]{2,1,0:T(8,128)(2,1)S(1)} %gather_ctx.1) | copy-start | bytes 6291460
  76.7 1.1 copy-start.13
  85.5 1.0 copy-start.10
  86.5 0.8 copy-start.18
  87.3 0.7 copy-start.22
  118.9 2.1 copy-start.2
  121.0 0.7 copy-start.15
  175.1 47.5 %copy-start.4 = (f32[128,1024]{1,0:T(8,128)S(1)}, f32[128,1024]{1,0:T(8,128)}, u32[]{:S(2)}) copy-start(f32[128,1024]{1,0:T(8,128)} %copy-done.3) | copy-start | bytes 1572868
  175.2 47.5 %copy-start.6 = (f32[128,1024]{1,0:T(8,128)S(1)}, f32[128,1024]{1,0:T(8,128)}, u32[]{:S(2)}) copy-start(f32[128,1024]{1,0:T(8,128)} %copy-done.5) | copy-start | bytes 1572868
  175.2 47.5 %copy-start.11 = (f32[8,256,1]{2,1,0:T(8,128)S(1)}, f32[8,256,1]{2,1,0:T(8,128)}, u32[]{:S(2)}) copy-start(f32[8,256,1]{2,1,0:T(8,128)} %copy-done.10) | copy-start | bytes 24580
  175.2 47.5 %copy-start.14 = (bf16[128,1024]{1,0:T(8,128)(2,1)S(1)}, bf16[128,1024]{1,0:T(8,128)(2,1)}, u32[]{:S(2)}) copy-start(bf16[128,1024]{1,0:T(8,128)(2,1)} %copy-done.12) | copy-start | bytes 786436
  175.2 47.5 %copy-start.16 = (bf16[128,1024]{1,0:T(8,128)(2,1)S(1)}, bf16[128,1024]{1,0:T(8,128)(2,1)}, u32[]{:S(2)}) copy-start(bf16[128,1024]{1,0:T(8,128)(2,1)} %copy-done.15) | copy-start | bytes 786436
  175.2 47.5 %copy-start.17 = (bf16[1,128,1024]{2,1,0:T(8,128)(2,1)S(1)}, bf16[1,128,1024]{2,1,0:T(8,128)(2,1)}, u32[]{:S(2)}) copy-start(bf16[1,128,1024]{2,1,0:T(8,128)(2,1)} %param.23) | copy-start | bytes 786436
  175.2 47.5 %copy-start.19 = (f32[128,1024]{1,0:T(8,128)S(1)}, f32[128,1024]{1,0:T(8,128)}, u32[]{:S(2)}) copy-start(f32[128,1024]{1,0:T(8,128)} %copy-done.18) | copy-start | bytes 1572868
  175.2 47.5 %copy-start.23 = (bf16[128,1024]{1,0:T(8,128)(2,1)S(1)}, bf16[128,1024]{1,0:T(8,128)(2,1)}, u32[]{:S(2)}) copy-start(bf16[128,1024]{1,0:T(8,128)(2,1)} %copy-done.22) | copy-start | bytes 786436
  222.7 85.0 %copy-start.21 = (bf16[128,1024]{1,0:T(8,128)(2,1)S(1)}, bf16[128,1024]{1,0:T(8,128)(2,1)}, u32[]{:S(2)}) copy-start(bf16[128,1024]{1,0:T(8,128)(2,1)} %copy-done.20) | copy-start | bytes 786436
  237.8 1.6 copy-start.9
  307.7 1.6 copy-start.8
Sparse Core Ops, SparseCore 0:
  10.5 53.3 all-gather.3
  66.3 59.0 all-gather.5
  175.3 67.9 reduce-scatter.1

commit v2 on v1

v2 whole, which is shorter than its diff:
```python
import jax
import jax.numpy as jnp
from jax import lax
from jax.experimental import pallas as pl
from jax.experimental.pallas import tpu as pltpu
from jax.sharding import PartitionSpec as P

MESH = pl.DeviceIdType.MESH
F32 = jnp.float32
BF16 = jnp.bfloat16
DH = 64
EPS = 1e-05
ROPE_BASE = 10000.0
MASKED = -1e30
VMEM = pl.BlockSpec(memory_space=pltpu.VMEM)
NT = (((1,), (1,)), ((), ()))
TN = (((0,), (0,)), ((), ()))


def dot(a, b, dims=(((1,), (0,)), ((), ()))):
    return lax.dot_general(a, b, dims, preferred_element_type=F32)


def wsh_place():
    w = lax.axis_index("wsh")
    return w // 4, (w // 2) % 2, w % 2


def wsh_slot(a, b, core):
    return (a * 2 + b) * 2 + core


def wsh_device(a, b, core):
    return (lax.axis_index("ctx"), wsh_slot(a, b, core))


def ctx_place():
    c = lax.axis_index("ctx")
    return c % 4, c // 4


def ctx_slot(a, b):
    return b * 4 + a


def ctx_device(a, b):
    return (ctx_slot(a, b), lax.axis_index("wsh"))


def around(a, step):
    return lax.rem(a + step, 4)


def greet(peers):
    barrier = pltpu.get_barrier_semaphore()
    for peer in peers:
        pl.semaphore_signal(barrier, inc=1, device_id=peer, device_id_type=MESH)
    pl.semaphore_wait(barrier, len(peers))


def remote(src, dst, send, recv, k, device):
    return pltpu.make_async_remote_copy(
        src_ref=src,
        dst_ref=dst,
        send_sem=send.at[k],
        recv_sem=recv.at[k],
        device_id=device,
        device_id_type=MESH,
    )


def wsh_peers():
    a, b, core = wsh_place()
    return [
        wsh_device(around(a, 1), b, core),
        wsh_device(around(a, 3), b, core),
        wsh_device(around(a, 2), b, core),
        wsh_device(a, 1 - b, core),
        wsh_device(a, b, 1 - core),
    ]


def ctx_peers():
    a, b = ctx_place()
    return [
        ctx_device(around(a, 1), b),
        ctx_device(around(a, 3), b),
        ctx_device(around(a, 2), b),
        ctx_device(a, 1 - b),
    ]


def run(*plans):
    plans = list(plans)
    while plans:
        plans = [p for p in plans if next(p, "end") != "end"]


def gather_plan(full, slot, device, a, b, send, recv, arrived=lambda *_: None):
    up, down, far = around(a, 1), around(a, 3), around(a, 2)
    other = 1 - b

    def push(k, sa, sb, to):
        at = full.at[slot(sa, sb)]
        copy = remote(at, at, send, recv, k, to)
        copy.start()
        return copy

    def landed(k, sa, sb):
        at = full.at[slot(sa, sb)]
        remote(at, at, send, recv, k, device(a, b)).wait_recv()
        arrived(k, sa, sb)

    sent = [
        push(3, a, b, device(a, other)),
        push(0, a, b, device(up, b)),
        push(1, a, b, device(down, b)),
        push(2, a, b, device(far, b)),
    ]
    yield
    landed(3, a, other)
    sent.append(push(4, a, other, device(up, b)))
    sent.append(push(5, a, other, device(down, b)))
    yield
    landed(0, down, b)
    landed(1, up, b)
    yield
    landed(2, far, b)
    sent.append(push(6, far, b, device(a, other)))
    yield
    landed(4, down, other)
    landed(5, up, other)
    yield
    landed(6, far, other)
    for copy in sent:
        copy.wait_send()


def gather_wsh_plan(full, sems, after_same=lambda: None):
    send, recv, send_c, recv_c = sems
    a, b, core = wsh_place()
    handed = []

    def hand(k, sa, sb):
        at = full.at[wsh_slot(sa, sb, core)]
        copy = remote(at, at, send_c, recv_c, k, wsh_device(a, b, 1 - core))
        copy.start()
        handed.append((copy, k, sa, sb))

    def take(k, sa, sb):
        at = full.at[wsh_slot(sa, sb, 1 - core)]
        remote(at, at, send_c, recv_c, k, wsh_device(a, b, 1 - core)).wait_recv()

    hand(7, a, b)
    slot = lambda sa, sb: wsh_slot(sa, sb, core)
    steps = gather_plan(full, slot, lambda sa, sb: wsh_device(sa, sb, core), a, b, send, recv, hand)
    for count, _ in enumerate(steps):
        if count == 3:
            near = [h for h in handed if h[1] in (7, 0, 1, 2)]
            for _, k, sa, sb in near:
                take(k, sa, sb)
            after_same()
        yield
    for copy, k, sa, sb in handed:
        if k not in (7, 0, 1, 2):
            take(k, sa, sb)
        copy.wait_send()


WSH_SEMS = [pltpu.SemaphoreType.DMA((7,))] * 2 + [pltpu.SemaphoreType.DMA((8,))] * 2
CTX_SEMS = [pltpu.SemaphoreType.DMA((7,))] * 2


def talk(kernel, outs, scratch, cid, name, in_specs, out_specs=None, limit=48, flops=0):
    return pl.pallas_call(
        kernel,
        out_shape=[jax.ShapeDtypeStruct(s, d) for s, d in outs],
        in_specs=in_specs,
        out_specs=out_specs or [VMEM] * len(outs),
        scratch_shapes=list(scratch),
        compiler_params=pltpu.CompilerParams(
            collective_id=cid, has_side_effects=True, vmem_limit_bytes=limit << 20
        ),
        cost_estimate=pl.CostEstimate(
            flops=flops, bytes_accessed=1 << 20, transcendentals=0
        ),
        name=name,
    )


def gather_weights(x, cid):
    rows, cols = x.shape

    def kernel(x_ref, full, *sems):
        a, b, core = wsh_place()
        greet(wsh_peers())
        full[wsh_slot(a, b, core)] = x_ref[...]
        run(gather_wsh_plan(full, sems))

    return talk(
        kernel, [((16, rows, cols), BF16)], WSH_SEMS, cid, "gather_weights", [VMEM], flops=20 << 30
    )(x)[0]


def gather_sequence(kv, cot, wo, cid):
    def kernel(kv_r, cot_r, wo_r, kv_full, cot_full, wo_full, *sems):
        a, b, core = wsh_place()
        ca, cb = ctx_place()
        greet(wsh_peers() + ctx_peers())
        kv_full[ctx_slot(ca, cb)] = kv_r[...]
        wo_full[wsh_slot(a, b, core)] = wo_r[...]
        cot_full[wsh_slot(a, b, core)] = cot_r[...]
        run(
            gather_plan(kv_full, ctx_slot, ctx_device, ca, cb, *sems[:2]),
            gather_wsh_plan(wo_full, sems[2:6]),
            gather_wsh_plan(cot_full, sems[6:10]),
        )

    return talk(
        kernel,
        [((8, 128, 1024), BF16), ((16, 128, 1024), BF16), ((16, 64, 1024), BF16)],
        CTX_SEMS + WSH_SEMS * 2,
        cid,
        "gather_sequence",
        [VMEM] * 3,
        flops=25 << 30,
    )(kv, cot, wo)


def scatter_plan(acc, land, slot, device, a, b, send, recv, ready, add):
    up, down, far = around(a, 1), around(a, 3), around(a, 2)
    other = 1 - b

    def push(k, sa, sb, to):
        copy = remote(acc.at[slot(sa, sb)], land.at[k], send, recv, k, to)
        copy.start()
        return copy

    def landed(k, sa, sb):
        remote(acc.at[slot(sa, sb)], land.at[k], send, recv, k, device(a, b)).wait_recv()
        add(sa, sb, k)

    sent = []
    ready(up, other)
    sent.append(push(1, up, other, device(up, b)))
    ready(far, other)
    sent.append(push(0, far, other, device(a, other)))
    ready(down, other)
    sent.append(push(2, down, other, device(down, b)))
    ready(a, other)
    ready(up, b)
    sent.append(push(3, up, b, device(up, b)))
    ready(far, b)
    ready(down, b)
    sent.append(push(4, down, b, device(down, b)))
    ready(a, b)
    yield
    landed(0, far, b)
    sent.append(push(5, far, b, device(far, b)))
    yield
    landed(1, a, other)
    landed(2, a, other)
    sent.append(push(6, a, other, device(a, other)))
    yield
    landed(3, a, b)
    landed(4, a, b)
    yield
    landed(5, a, b)
    landed(6, a, b)
    for copy in sent:
        copy.wait_send()


def pair_slot(sa, sb):
    return sa * 2 + sb


def hand_step(k):
    a, b, _ = wsh_place()
    return lax.rem(a + k + 1, 4), lax.rem(b + 1 + k // 4, 2)


def hand_over(p_ref, land_c, send_c, recv_c, k):
    a, b, core = wsh_place()
    return remote(
        p_ref.at[pair_slot(*hand_step(k)), 1 - core],
        land_c.at[k],
        send_c,
        recv_c,
        k,
        wsh_device(a, b, 1 - core),
    )


def scatter_wsh_plan(p_ref, acc, land, land_c, sems, handed=False):
    send, recv, send_c, recv_c = sems
    a, b, core = wsh_place()
    copies = [hand_over(p_ref, land_c, send_c, recv_c, k) for k in range(8)]
    if not handed:
        for copy in copies:
            copy.start()
    count = [0]

    def ready(sa, sb):
        k = count[0]
        count[0] += 1
        copies[k].wait_recv()
        at = pair_slot(sa, sb)
        acc[at] = (p_ref[at, core].astype(F32) + land_c[k].astype(F32)).astype(acc.dtype)

    def add(sa, sb, k):
        at = pair_slot(sa, sb)
        acc[at] = (acc[at].astype(F32) + land[k].astype(F32)).astype(acc.dtype)

    device = lambda sa, sb: wsh_device(sa, sb, core)
    yield from scatter_plan(acc, land, pair_slot, device, a, b, send, recv, ready, add)
    for copy in copies:
        copy.wait_send()


def scatter_ctx_plan(p_ref, acc, land, sems):
    a, b = ctx_place()

    def ready(sa, sb):
        at = ctx_slot(sa, sb)
        acc[at] = p_ref[at]

    def add(sa, sb, k):
        at = ctx_slot(sa, sb)
        acc[at] = (acc[at].astype(F32) + land[k].astype(F32)).astype(acc.dtype)

    yield from scatter_plan(acc, land, ctx_slot, ctx_device, a, b, *sems, ready, add)


def wsh_land(rows, cols):
    return [
        pltpu.VMEM((8, rows, cols), BF16),
        pltpu.VMEM((7, rows, cols), BF16),
        pltpu.VMEM((8, rows, cols), BF16),
    ]


def sum_sequence(gkv, pay, cid):
    def kernel(gkv_r, pay_r, gkv_o, pay_o, kacc, kland, acc, land, land_c, *sems):
        greet(wsh_peers() + ctx_peers())
        run(
            scatter_ctx_plan(gkv_r, kacc, kland, sems[:2]),
            scatter_wsh_plan(pay_r, acc, land, land_c, sems[2:]),
        )
        a, b, _ = wsh_place()
        pay_o[...] = acc[pair_slot(a, b)]
        gkv_o[...] = kacc[lax.axis_index("ctx")]

    return talk(
        kernel,
        [((128, 1024), BF16), ((128, 1024), BF16)],
        [pltpu.VMEM((8, 128, 1024), BF16), pltpu.VMEM((7, 128, 1024), BF16)]
        + wsh_land(128, 1024)
        + CTX_SEMS
        + WSH_SEMS,
        cid,
        "sum_sequence",
        [VMEM] * 2,
        flops=25 << 30,
    )(gkv, pay.reshape(8, 2, 128, 1024))


def sum_all(p, cid):
    _, rows, cols = p.shape
    part = rows // 8

    def kernel(p_ref, o_ref, acc, land, land_c, acc2, land2, *sems):
        greet(wsh_peers() + ctx_peers())
        run(scatter_wsh_plan(p_ref, acc, land, land_c, sems[:4]))
        wa, wb, _ = wsh_place()
        acc2[...] = acc[pair_slot(wa, wb)].astype(F32).reshape(8, part, cols)
        a, b = ctx_place()

        def add(sa, sb, k):
            acc2[ctx_slot(sa, sb)] += land2[k]

        none = lambda *_: None
        run(scatter_plan(acc2, land2, ctx_slot, ctx_device, a, b, *sems[4:6], none, add))
        o_ref[ctx_slot(a, b)] = acc2[ctx_slot(a, b)]
        run(gather_plan(o_ref, ctx_slot, ctx_device, a, b, *sems[6:8]))

    return talk(
        kernel,
        [((8, part, cols), F32)],
        wsh_land(rows, cols)
        + [pltpu.VMEM((8, part, cols), F32), pltpu.VMEM((7, part, cols), F32)]
        + WSH_SEMS
        + CTX_SEMS * 2,
        cid,
        "sum_all",
        [VMEM],
        flops=50 << 30,
    )(p.reshape(8, 2, rows, cols))[0].reshape(rows, cols)


def compute(kernel, outs, scratch=(), limit=48, name=None):
    return pl.pallas_call(
        kernel,
        out_shape=[jax.ShapeDtypeStruct(s, d) for s, d in outs],
        scratch_shapes=list(scratch),
        compiler_params=pltpu.CompilerParams(vmem_limit_bytes=limit << 20),
        cost_estimate=pl.CostEstimate(flops=10 << 30, bytes_accessed=1 << 20, transcendentals=0),
        name=name,
    )


def rms_scale(x):
    return lax.rsqrt(jnp.mean(x * x, -1, keepdims=True) + EPS)


def norm_back(u, x, scale):
    return scale * u - x * scale * scale * scale * jnp.mean(u * x, -1, keepdims=True)


def low_half(shape):
    return lax.broadcasted_iota(jnp.int32, shape, len(shape) - 1) % DH < DH // 2


def rotate(v, cos, sin):
    width = v.shape[-1]
    turned = jnp.where(
        low_half(v.shape), -pltpu.roll(v, width - DH // 2, 1), pltpu.roll(v, DH // 2, 1)
    )
    return v * cos + turned * sin


def unrotate(v, cos, sin):
    width = v.shape[-1]
    scaled = v * sin
    turned = jnp.where(
        low_half(v.shape), pltpu.roll(scaled, width - DH // 2, 1), -pltpu.roll(scaled, DH // 2, 1)
    )
    return v * cos + turned


def project_kernel(tok, w, cos, sin, normed_o, q_o, kv_o, misc_o):
    x = tok[...].astype(F32)
    misc = w[:, 2048:2176].astype(F32).T
    misc_o[...] = misc
    normed = (x * rms_scale(x) * misc[96:97]).astype(BF16)
    normed_o[...] = normed
    c, s = cos[...], sin[...]
    q = dot(normed, w[:, :1024])
    q_o[...] = rotate(q, c, s).astype(BF16)
    k = dot(normed, w[:, 1024:1536])
    kv_o[:, :512] = rotate(k, c[:, :512], s[:, :512]).astype(BF16)
    kv_o[:, 512:] = dot(normed, w[:, 1536:2048]).astype(BF16)


def two_heads(ref, g):
    return jnp.concatenate(
        [ref[:, g * 128 : g * 128 + 64], ref[:, g * 128 + 64 : g * 128 + 128]], 0
    )


def side_by_side(rows):
    return jnp.concatenate([rows[:128], rows[128:]], 1)


def visible_mask():
    row = lax.broadcasted_iota(jnp.int32, (256, 1024), 0) % 128
    col = lax.broadcasted_iota(jnp.int32, (256, 1024), 1)
    return col <= row + lax.axis_index("ctx") * 128


def attend_kernel(q, kv, tok, wo, misc, merged_o, mid_o, normed_o, lse_o):
    visible = visible_mask()
    for g in range(8):
        keys = kv[:, g * 64 : g * 64 + 64]
        values = kv[:, 512 + g * 64 : 512 + g * 64 + 64]
        scores = jnp.where(visible, dot(two_heads(q, g), keys, NT) * DH**-0.5, MASKED)
        top = jnp.max(scores, -1, keepdims=True)
        raised = jnp.exp(scores - top)
        total = jnp.sum(raised, -1, keepdims=True)
        lse_o[g] = top + jnp.log(total)
        probs = (raised * (1.0 / total)).astype(BF16)
        merged_o[:, g * 128 : g * 128 + 128] = side_by_side(dot(probs, values)).astype(BF16)
    mid = tok[...].astype(F32) + dot(merged_o[...], wo[...])
    mid_o[...] = mid
    normed_o[...] = (mid * rms_scale(mid) * misc[97:98, :]).astype(BF16)


def parts_of(v):
    high = v.astype(BF16)
    rest = v - high.astype(F32)
    middle = rest.astype(BF16)
    return high, middle, (rest - middle.astype(F32)).astype(BF16)


def experts_kernel(
    x_r, cot, w_in_r, w_out_r, misc, mask, full, back_o, wg0, wg1, wg2, wg3,
    w_in, w_out, sel, buf, gbuf, gcol, ggcol, gp, hidden, gact, gcopy, pay, wg,
    acc, land, land_c, load, store, *sems,
):
    loads = [
        pltpu.make_async_copy(cot, gp, load.at[0]),
        pltpu.make_async_copy(w_in_r, w_in, load.at[1]),
        pltpu.make_async_copy(w_out_r, w_out, load.at[2]),
    ]
    for copy in loads:
        copy.start()
    wa, wb, core = wsh_place()
    ca, cb = ctx_place()
    own = lax.axis_index("wsh") * 2
    tri = (
        lax.broadcasted_iota(jnp.int32, (128, 128), 0)
        < lax.broadcasted_iota(jnp.int32, (128, 128), 1)
    ).astype(BF16)
    router = misc[0:32, :].astype(BF16)
    experts = lax.broadcasted_iota(jnp.int32, (32, 128), 0)
    slots = lax.broadcasted_iota(jnp.int32, (64, 128), 0).astype(F32)

    def pick(b):
        def one(i, _):
            s = wsh_slot(lax.rem(wa + i // 2, 4), b, i % 2)
            chosen = mask[s]
            x = full[s]
            logits = jnp.where(chosen > 0, dot(router, x, NT), MASKED)
            raised = jnp.exp(logits - jnp.max(logits, 0, keepdims=True)) * chosen
            gates = raised / jnp.sum(raised, 0, keepdims=True)
            earlier = dot(chosen.astype(BF16), tri)
            place, gate = [], []
            for j in range(2):
                is_own = experts == own + j
                row = lambda v: jnp.sum(jnp.where(is_own, v, 0.0), 0, keepdims=True)
                hit = (slots == row(earlier)) & (row(chosen) > 0)
                place.append(hit.astype(F32))
                gate.append(jnp.sum(jnp.where(hit, row(gates), 0.0), 1, keepdims=True))
            both = jnp.concatenate(place, 0).astype(BF16)
            sel[s] = both
            xb = dot(both, x).astype(BF16)
            gb = dot(both, gp[pl.ds(pl.multiple_of(s * 128, 128), 128), :]).astype(BF16)
            at = pl.ds(pl.multiple_of(s * 64, 64), 64)
            for j in range(2):
                buf[j, at, :] = xb[j * 64 : j * 64 + 64]
                gbuf[j, at, :] = gb[j * 64 : j * 64 + 64]
                gcol[j, at, :] = gate[j]
            return _

        lax.fori_loop(0, 8, one, 0)

    greet(wsh_peers())
    full[wsh_slot(wa, wb, core)] = x_r[...]

    def pick_same():
        loads[0].wait()
        pick(wb)

    run(gather_wsh_plan(full, sems[:4], pick_same))
    pick(1 - wb)
    loads[1].wait()
    loads[2].wait()

    def tile(i, _):
        j = i // 4
        at = pl.ds(pl.multiple_of((i % 4) * 256, 256), 256)
        flat = pl.ds(pl.multiple_of(i * 256, 256), 256)
        act = dot(buf[j, at, :], w_in[j], NT)
        gate, up = act[:, :512], act[:, 512:]
        s = jax.nn.sigmoid(gate)
        h = (gate * s * up).astype(BF16)
        hidden[j, at, :] = h
        produced = dot(h, w_out[j], NT).astype(BF16).astype(F32)
        gate_col = gcol[j, at, :]
        gr = gbuf[j, at, :].astype(F32)
        ggcol[j, at, :] = jnp.sum(gr * produced, 1, keepdims=True)
        gbuf[j, at, :] = (produced * gate_col).astype(BF16)
        gpt = (gr * gate_col).astype(BF16)
        gp[flat, :] = gpt
        gh = dot(gpt, w_out[j])
        ga_gate = (gh * up * s * (1.0 + gate * (1.0 - s))).astype(BF16)
        ga_up = (gh * gate * s).astype(BF16)
        ga = jnp.concatenate([ga_gate, ga_up], 1)
        gact[j, at, :] = ga
        gcopy[j, at, :] = dot(ga, w_in[j]).astype(BF16)
        return _

    lax.fori_loop(0, 8, tile, 0)
    lane = lax.broadcasted_iota(jnp.int32, (64, 128), 1)

    def rows(ref, s):
        at = pl.ds(pl.multiple_of(s * 64, 64), 64)
        return jnp.concatenate([ref[0, at, :], ref[1, at, :]], 0)

    def combine(k, _):
        sa, sb = hand_step(k)
        for c in range(2):
            s = wsh_slot(sa, sb, c)
            at = pl.ds(pl.multiple_of(s * 64, 64), 64)
            both = sel[s]
            pay[pair_slot(sa, sb), c, :, :1024] = dot(both, rows(gcopy, s), TN).astype(BF16)
            cells = []
            for j in range(2):
                cell = jnp.zeros((64, 128), F32)
                for n, part in enumerate(parts_of(ggcol[j, at, :])):
                    cell = jnp.where(lane == own + j + 32 * n, part.astype(F32), cell)
                cells.append(cell.astype(BF16))
            pay[pair_slot(sa, sb), c, :, 1024:] = dot(both, jnp.concatenate(cells, 0), TN).astype(
                BF16
            )
        hand_over(pay, land_c, sems[6], sems[7], k).start()
        return _

    lax.fori_loop(0, 8, combine, 0)

    stores = [
        pltpu.make_async_copy(wg.at[d], out, store.at[d])
        for d, out in enumerate((wg0, wg1, wg2, wg3))
    ]

    def weights(i, _):
        d, j = i // 2, i % 2
        blocks = [
            pl.ds(pl.multiple_of(ctx_slot(lax.rem(ca + d, 4), lax.rem(cb + e, 2)) * 128, 128), 128)
            for e in range(2)
        ]
        lhs = jnp.concatenate([gact[j, :, blk] for blk in blocks], 1)
        gi = dot(lhs, buf[j], TN).astype(BF16)
        here = pl.ds(pl.multiple_of(j * 1024, 1024), 1024)
        lhs = jnp.concatenate([gp[here, blk] for blk in blocks], 1)
        go = dot(lhs, hidden[j], TN).astype(BF16)
        for e in range(2):
            wg[d, e, j, :, :1024] = gi[e * 128 : e * 128 + 128]
            wg[d, e, j, :, 1024:] = go[e * 128 : e * 128 + 128]
        return _

    def out_rows(s, _):
        full[s] = dot(sel[s], rows(gbuf, s), TN).astype(BF16)
        return _

    steps = scatter_wsh_plan(pay, acc, land, land_c, sems[4:8], handed=True)
    next(steps)
    lax.fori_loop(0, 4, weights, 0)
    stores[0].start()
    stores[1].start()
    next(steps)
    next(steps)
    lax.fori_loop(4, 8, weights, 0)
    stores[2].start()
    stores[3].start()
    next(steps)
    lax.fori_loop(0, 16, out_rows, 0)
    run(steps)
    back_o[...] = acc[pair_slot(wa, wb)]
    for copy in stores:
        copy.wait()


def experts(x, cot, w_in, w_out, misc, mask, cid):
    t, d, e = 128, 1024, 1024
    wg = ((2, 2, t, 1536), BF16)
    return talk(
        experts_kernel,
        [((16, t, d), BF16), ((t, 1152), BF16), wg, wg, wg, wg],
        [
            pltpu.VMEM((2, e, d), BF16),
            pltpu.VMEM((2, d, 512), BF16),
            pltpu.VMEM((16, 128, 128), BF16),
            pltpu.VMEM((2, e, d), BF16),
            pltpu.VMEM((2, e, d), BF16),
            pltpu.VMEM((2, e, 1), F32),
            pltpu.VMEM((2, e, 1), F32),
            pltpu.VMEM((2 * e, d), BF16),
            pltpu.VMEM((2, e, 512), BF16),
            pltpu.VMEM((2, e, d), BF16),
            pltpu.VMEM((2, e, d), BF16),
            pltpu.VMEM((8, 2, t, 1152), BF16),
            pltpu.VMEM((4, 2, 2, t, 1536), BF16),
        ]
        + wsh_land(t, 1152)
        + [pltpu.SemaphoreType.DMA((3,)), pltpu.SemaphoreType.DMA((4,))]
        + WSH_SEMS * 2,
        cid,
        "experts",
        [VMEM] + [pl.BlockSpec(memory_space=pl.ANY)] * 3 + [VMEM] * 2,
        [VMEM] * 2 + [pl.BlockSpec(memory_space=pl.ANY)] * 4,
        limit=63,
        flops=80 << 30,
    )(x, cot, w_in, w_out, misc, mask)


def split_dot(a, b, dims):
    high = a.astype(BF16)
    rest = (a - high.astype(F32)).astype(BF16)
    return dot(high, b, dims) + dot(rest, b, dims)


def back_kernel(
    back, mid_r, cot, misc, mask, normed, merged, q, kv, lse, wo, cos, sin,
    gmid_o, gkv_o, gq_o, gwo_o, gmisc_o, gm, dkv,
):
    mid = mid_r[...]
    cells = back[:, 1024:].astype(F32)
    ggates = cells[:, :32] + cells[:, 32:64] + cells[:, 64:96]
    router = misc[0:32, :].astype(BF16)
    chosen = mask[...]
    logits = jnp.where(chosen > 0, dot(normed[...], router, NT), MASKED)
    raised = jnp.exp(logits - jnp.max(logits, 1, keepdims=True)) * chosen
    gates = raised / jnp.sum(raised, 1, keepdims=True)
    glogits = gates * (ggates - jnp.sum(gates * ggates, 1, keepdims=True))
    scale = rms_scale(mid)
    gnormed = back[:, :1024].astype(F32) + split_dot(glogits, router, (((1,), (0,)), ((), ())))
    gmisc_o[0:32, :] = split_dot(glogits, normed[...], TN)
    gmisc_o[32:33, :] = jnp.sum(gnormed * mid * scale, 0, keepdims=True)
    gmid = cot[...].astype(F32) + norm_back(gnormed * misc[97:98, :], mid, scale)
    gmid_o[...] = gmid
    branch = gmid.astype(BF16)
    gwo_o[...] = dot(merged[...], branch, TN).astype(BF16)
    gm[...] = dot(branch, wo[...], NT).astype(BF16)
    visible = visible_mask()
    gq = []
    for g in range(8):
        keys = kv[:, g * 64 : g * 64 + 64]
        values = kv[:, 512 + g * 64 : 512 + g * 64 + 64]
        queries, grads = two_heads(q, g), two_heads(gm, g)
        scores = jnp.where(visible, dot(queries, keys, NT) * DH**-0.5, MASKED)
        probs = jnp.exp(scores - lse[g])
        gprobs = dot(grads, values, NT)
        inner = jnp.sum(probs * gprobs, -1, keepdims=True)
        graw = (probs * (gprobs - inner) * DH**-0.5).astype(BF16)
        gq.append(side_by_side(dot(graw, keys)))
        dkv[g * 64 : g * 64 + 64, :] = dot(queries, graw, TN)
        dkv[512 + g * 64 : 512 + g * 64 + 64, :] = dot(grads, probs.astype(BF16), TN)
    gq_o[...] = unrotate(jnp.concatenate(gq, 1), cos[...], sin[...]).astype(BF16)
    for c in range(8):
        gkv_o[c] = dkv[:, c * 128 : c * 128 + 128].T.astype(BF16)


def finish_kernel(
    gkv, gq, normed, w, tok, gmid, cos, sin, misc, gwo, gmisc, mid, extra,
    tgrad_o, pack_o, out_o, gall,
):
    out_o[...] = (mid[...] + extra[...].astype(F32)).astype(BF16)
    c, s = cos[:, :512], sin[:, :512]
    gall[:, :1024] = gq[...]
    gall[:, 1024:1536] = unrotate(gkv[:, :512].astype(F32), c, s).astype(BF16)
    gall[:, 1536:] = gkv[:, 512:]
    x = tok[...].astype(F32)
    scale = rms_scale(x)
    gnormed = dot(gall[...], w[:, :2048], NT)
    pack_o[:, :2048] = dot(normed[...], gall[...], TN).astype(BF16)
    pack_o[:, 2048:3072] = gwo[...]
    gain = jnp.sum(gnormed * x * scale, 0, keepdims=True)
    rows = jnp.concatenate([gmisc[0:33, :], gain, jnp.zeros((94, 1024), F32)], 0)
    pack_o[:, 3072:] = rows.T.astype(BF16)
    tgrad_o[...] = (gmid[...] + norm_back(gnormed * misc[96:97, :], x, scale)).astype(BF16)


def local(
    tokens, gain_attn, w_query, w_key, w_value, w_output, gain_moe, w_router, w_in, w_out, routes,
    cotangent,
):
    tok = tokens.reshape(128, 1024)
    cot = cotangent.reshape(128, 1024)
    chosen = routes.reshape(128, 8)
    own_mask = jnp.sum(
        (chosen[:, :, None] == jnp.arange(32, dtype=jnp.int32)).astype(F32), 1
    )
    low_mask = own_mask.astype(BF16)
    pack = jnp.concatenate(
        [
            w_query, w_key, w_value, w_router, low_mask[:64], low_mask[64:],
            gain_attn[:, None], gain_moe[:, None], jnp.zeros((64, 30), BF16),
        ],
        1,
    )
    positions = (lax.axis_index("ctx") * 128 + jnp.arange(128, dtype=jnp.int32)).astype(F32)
    frequencies = ROPE_BASE ** (-jnp.arange(DH // 2, dtype=F32) * 2.0 / DH)
    angles = positions[:, None] * frequencies[None, :]
    cos = jnp.tile(jnp.cos(angles), (1, 32))
    sin = jnp.tile(jnp.sin(angles), (1, 32))

    w = gather_weights(pack, 0).reshape(1024, 2176)
    t, d = 128, 1024
    normed, q, kv, misc = compute(
        project_kernel,
        [((t, d), BF16), ((t, d), BF16), ((t, d), BF16), ((128, d), F32)],
        name="project",
    )(tok, w, cos, sin)
    kv_all, cot_all, wo = gather_sequence(kv, cot, w_output, 1)
    kv_all, cot_all, wo = kv_all.reshape(d, d), cot_all.reshape(2048, d), wo.reshape(d, d)
    merged, mid, normed_moe, lse = compute(
        attend_kernel,
        [((t, d), BF16), ((t, d), F32), ((t, d), BF16), ((8, 256, 1), F32)],
        name="attend",
    )(q, kv_all, tok, wo, misc)
    mask = misc[32:96].reshape(2, 32, 16, 64).transpose(2, 1, 0, 3).reshape(16, 32, 128)
    pay, back, *wg = experts(normed_moe, cot_all, w_in, w_out, misc, mask, 2)

    def along_x(step):
        return [(c, c // 4 * 4 + (c + step) % 4) for c in range(8)]

    met = [lax.ppermute(wg[step], "ctx", along_x(step)) for step in (1, 2, 3)]
    chip_sum = wg[0].astype(F32) + met[0].astype(F32) + met[1].astype(F32) + met[2].astype(F32)
    across = lax.ppermute(chip_sum[1].astype(BF16), "ctx", [(c, (c + 4) % 8) for c in range(8)])
    expert_grads = chip_sum[0] + across.astype(F32)

    gmid, gkv, gq, gwo, gmisc = compute(
        back_kernel,
        [((t, d), F32), ((8, t, d), BF16), ((t, d), BF16), ((d, d), BF16), ((40, d), F32)],
        [pltpu.VMEM((t, d), BF16), pltpu.VMEM((d, d), F32)],
        name="back",
    )(back, mid, cot, misc, own_mask, normed_moe, merged, q, kv_all, lse, wo, cos, sin)
    gkv_own, extra = sum_sequence(gkv, pay, 3)
    tokens_grad, packed, output = compute(
        finish_kernel,
        [((t, d), BF16), ((d, 3200), BF16), ((t, d), BF16)],
        [pltpu.VMEM((t, 2048), BF16)],
        name="finish",
    )(gkv_own, gq, normed, w, tok, gmid, cos, sin, misc, gwo, gmisc, mid, extra)
    sums = sum_all(packed.reshape(16, 64, 3200), 4)
    return (
        output.reshape(1, 128, 1024),
        tokens_grad.reshape(1, 128, 1024),
        sums[:, 3105],
        sums[:, :1024],
        sums[:, 1024:1536],
        sums[:, 1536:2048],
        sums[:, 2048:3072],
        sums[:, 3104],
        sums[:, 3072:3104],
        expert_grads[:, :, :1024],
        expert_grads[:, :, 1024:],
    )


def solution(mesh):
    return jax.shard_map(
        local,
        mesh=mesh,
        in_specs=(
            P("wsh", "ctx", None),
            P("wsh"),
            P("wsh", None),
            P("wsh", None),
            P("wsh", None),
            P("wsh", None),
            P("wsh"),
            P("wsh", None),
            P("wsh", None, None),
            P("wsh", None, None),
            P("wsh", "ctx", None, None),
            P("wsh", "ctx", None),
        ),
        out_specs=(
            P("wsh", "ctx", None),
            P("wsh", "ctx", None),
            P("wsh"),
            P("wsh", None),
            P("wsh", None),
            P("wsh", None),
            P("wsh", None),
            P("wsh"),
            P("wsh", None),
            P("wsh", "ctx", None),
            P("wsh", "ctx", None),
        ),
        check_vma=False,
    )
```

time: 388 us -> 339 us (0.87)
  Pallas kernels: 339 us -> 297 us
  between operations: 14.2 us -> 1.02 us
  starting transfers between devices: 0.11 us -> 5.78 us
  waiting for transfers between devices: 5.13 us -> 0.01 us
  local copies, waits for them, and re-layouts: 25.3 us -> 29.9 us
    pallas_call x9 -> x7, Pallas kernels: 328 us -> 286 us  [the longest x1 75.6 us: experts(): talk(experts_kernel, [((16, t, d), BF16), ((t, 1152), BF16), wg, wg, wg,...]
    ppermute x0 -> x4, starting transfers between devices: none -> 5.78 us  [the longest x3 5.02 us: local(): met = [lax.ppermute(wg[step], 'ctx', along_x(step)) for step in (1, 2, 3)]]
    unnamed x54 -> x70, local copies, waits for them, and re-layouts: 16.2 us -> 20.9 us
  transfers between devices with their start and end apart: 3 -> 4, of which waited for: 1 -> 0; matrix products, arithmetic and copies ran while one was open for 2% -> 1% of each run, Pallas kernels for 75% -> 42%
where the time goes in v2:
time: 339 us; the launch traced here: 337 us
  Pallas kernels  297 us (88%)
  local copies, waits for them, and re-layouts  29.9 us (9%)
  starting transfers between devices  5.78 us (2%)
    pallas_call x1, Pallas kernels, experts(): talk(experts_kernel, [((16, t, d), BF16), ((t, 1152), BF16), wg, wg, wg,...  75.6 us
    pallas_call x1, Pallas kernels, sum_sequence(): talk(kernel, [((128, 1024), BF16), ((128, 1024), BF16)], [pltpu.VMEM((8,...  63.1 us
    pallas_call x1, Pallas kernels, sum_all(): talk(kernel, [((8, part, cols), F32)], wsh_land(rows, cols) + [pltpu.VMEM...  56.9 us
    pallas_call x1, Pallas kernels, gather_sequence(): talk(kernel, [((8, 128, 1024), BF16), ((16, 128, 1024), BF16), ((16, 64,...  39 us
    pallas_call x1, Pallas kernels, gather_weights(): talk(kernel, [((16, rows, cols), BF16)], WSH_SEMS, cid, 'gather_weights',...  28.5 us
    unnamed x70, local copies, waits for them, and re-layouts  20.9 us
    pallas_call x1, Pallas kernels, local(): compute(back_kernel, [((t, d), F32), ((8, t, d), BF16), ((t, d), BF16), (...  14.6 us
    pallas_call x1, Pallas kernels, local(): compute(finish_kernel, [((t, d), BF16), ((d, 3200), BF16), ((t, d), BF16)...  8.2 us
  transfers between devices with their start and end apart: 4, of which 0 were waited for; matrix products, arithmetic and copies ran while one was open for 1% of the time, Pallas kernels for 42%

profile of v2, /device:TPU:2, one launch (start us, length us, event | category | flops | bytes accessed | tf_op | source)
XLA Modules:
  0.0 336.7 jit_solution(6350572344292298559)
XLA Ops:
  3.8 1.1 concatenate.3.x_ref
  4.9 28.5 %gather_weights.1 = bf16[16,64,2176]{2,1,0:T(8,128)(2,1)S(1)} custom-call(bf16[64,2176]{1,0:T(8,128)(2,1)S(1)} %concatenate.3.x_ref), custom_call_target="tpu_custom_call" | custom-call | flops 21474836480 | bytes 1048576 | tf_op jit(solution)/shard_map/gather_weights/pallas_call | solution.py:200
  33.4 2.1 copy-done.12
  36.5 3.2 project.1
  41.0 1.0 reshape.137.mask
  42.0 39.0 %gather_sequence.1 = (bf16[8,128,1024]{2,1,0:T(8,128)(2,1)S(1)}, bf16[16,128,1024]{2,1,0:T(8,128)(2,1)}, bf16[16,64,1024]{2,1,0:T(8,128)(2,1)S(1)}) custom-call(bf16[128,1024]{1,0:T(8,128)(2,1)S(1)} %get-tuple-element.39.kv_r, bf16[128,1024]{1,0:T(8,128)(2,1)S(1)} %bitcast.29, bf16[64,1024]{1,0:T(8,128)(2,1)S(1)} %copy-done.11), custom_call_target="tpu_custom_call" | custom-call | flops 26843545600 | bytes 1048576 | tf_op jit(solution)/shard_map/gather_sequence/pallas_call | solution.py:219
  81.0 1.4 copy-done.14
  82.4 1.1 copy-done.26
  83.5 7.7 %attend.1 = (bf16[128,1024]{1,0:T(8,128)(2,1)S(1)}, f32[128,1024]{1,0:T(8,128)S(1)}, bf16[128,1024]{1,0:T(8,128)(2,1)S(1)}, f32[8,256,1]{2,1,0:T(8,128)S(1)}) custom-call(bf16[128,1024]{1,0:T(8,128)(2,1)S(1)} %copy-done.26, bf16[1024,1024]{1,0:T(8,128)(2,1)S(1)} %bitcast.36, bf16[128,1024]{1,0:T(8,128)(2,1)S(1)} %bitcast.32, bf16[1024,1024]{1,0:T(8,128)(2,1)} %bitcast.38, ...), custom_call_target="tpu_custom_call" | custom-call | flops 10737418240 | bytes 1048576 | tf_op jit(solution)/shard_map/attend/pallas_call | solution.py:787
  91.2 1.0 copy-done.17
  92.2 0.8 copy-done.19
  94.5 75.6 %experts.1 = (bf16[16,128,1024]{2,1,0:T(8,128)(2,1)}, bf16[128,1152]{1,0:T(8,128)(2,1)}, bf16[2,2,128,1536]{3,2,1,0:T(8,128)(2,1)}, bf16[2,2,128,1536]{3,2,1,0:T...) custom-call(bf16[128,1024]{1,0:T(8,128)(2,1)} %copy-done.30, ...), custom_call_target="tpu_custom_call" | custom-call | flops 85899345920 | bytes 1048576 | tf_op jit(solution)/shard_map/experts/pallas_call | solution.py:657
  170.0 1.7 collective-permute-start
  171.8 1.8 collective-permute-start.1
  173.6 1.5 collective-permute-start.2
  175.1 1.0 copy-done.1
  176.1 1.0 copy-done.6
  177.2 1.2 copy-done.18
  178.4 1.0 copy-done.20
  179.4 1.0 copy-done.24
  180.4 0.9 copy-done.27
  181.3 0.9 copy-done.29
  182.3 0.9 copy-done.31
  183.2 14.6 %back.1 = (f32[128,1024]{1,0:T(8,128)S(1)}, bf16[8,128,1024]{2,1,0:T(8,128)(2,1)}, bf16[128,1024]{1,0:T(8,128)(2,1)S(1)}, bf16[1024,1024]{1,0:T(8,128)(2,1)}, f32[40,1024]{1,0:T(8,128)S(1)}) custom-call(bf16[128,1152]{1,0:T(8,128)(2,1)S(1)} %copy-done.24, f32[128,1024]{1,0:T(8,128)S(1)} %copy-done.20, bf16[128,1024]{1,0:T(8,128)(2,1)S(1)} %bitcast.30, ...), custom_call_target="tpu_custom_call" | custom-call | flops 10737418240 | bytes 1048576 | tf_op jit(solution)/shard_map/back/pallas_call | solution.py:803
  197.8 1.6 copy-done.16
  199.4 63.1 %sum_sequence.1 = (bf16[128,1024]{1,0:T(8,128)(2,1)S(1)}, bf16[128,1024]{1,0:T(8,128)(2,1)S(1)}) custom-call(bf16[8,128,1024]{2,1,0:T(8,128)(2,1)S(1)} %copy-done.16, bf16[8,2,128,1024]{3,2,1,0:T(8,128)(2,1)} %bitcast.47), custom_call_target="tpu_custom_call" | custom-call | flops 26843545600 | bytes 1048576 | tf_op jit(solution)/shard_map/sum_sequence/pallas_call | solution.py:354
  262.6 8.2 %finish.1 = (bf16[128,1024]{1,0:T(8,128)(2,1)}, bf16[1024,3200]{1,0:T(8,128)(2,1)}, bf16[128,1024]{1,0:T(8,128)(2,1)}) custom-call(bf16[128,1024]{1,0:T(8,128)(2,1)S(1)} %get-tuple-element.51.gkv, bf16[128,1024]{1,0:T(8,128)(2,1)S(1)} %get-tuple-element.52.gq, bf16[128,1024]{1,0:T(8,128)(2,1)S(1)} %copy-done.23, bf16[1024,2176]{1,0:T(8,128)(2,1)} %bitcast.35, ...), custom_call_target="tpu_custom_call" | custom-call | flops 10737418240 | bytes 1048576 | tf_op jit(solution)/shard_map/finish/pallas_call | solution.py:810
  272.5 0.8 copy-done.32
  273.3 56.9 %sum_all.1 = f32[8,8,3200]{2,1,0:T(8,128)S(1)} custom-call(bf16[8,2,64,3200]{3,2,1,0:T(8,128)(2,1)} %bitcast.46), custom_call_target="tpu_custom_call" | custom-call | flops 53687091200 | bytes 1048576 | tf_op jit(solution)/shard_map/sum_all/pallas_call | solution.py:387
  332.3 0.8 fusion.2
  333.2 1.6 fusion
  334.8 1.1 slice.68
  (83 shorter events, 11.4 us)
Async XLA Ops:
  1.5 2.4 copy-start.3
  33.4 2.2 copy-start.12
  35.5 0.9 copy-start.9
  36.2 3.5 %copy-start = (f32[128,1024]{1,0:T(8,128)}, f32[128,1024]{1,0:T(8,128)S(1)}, u32[]{:S(2)}) copy-start(f32[128,1024]{1,0:T(8,128)S(1)} %copy.46.sin) | copy-start | bytes 1572868
  40.4 40.7 %copy-start.25 = (bf16[128,1024]{1,0:T(8,128)(2,1)}, bf16[128,1024]{1,0:T(8,128)(2,1)S(1)}, u32[]{:S(2)}) copy-start(bf16[128,1024]{1,0:T(8,128)(2,1)S(1)} %get-tuple-element.38.q) | copy-start | bytes 786436
  40.4 42.0 %copy-start.5 = (f32[128,1024]{1,0:T(8,128)}, f32[128,1024]{1,0:T(8,128)S(1)}, u32[]{:S(2)}) copy-start(f32[128,1024]{1,0:T(8,128)S(1)} %get-tuple-element.42.misc) | copy-start | bytes 1572868
  40.4 1.6 copy-start.8
  40.4 1.6 copy-start.11
  81.0 1.4 copy-start.14
  82.4 8.8 %copy-start.13 = (bf16[8,128,1024]{2,1,0:T(8,128)(2,1)}, bf16[8,128,1024]{2,1,0:T(8,128)(2,1)S(1)}, u32[]{:S(2)}) copy-start(bf16[8,128,1024]{2,1,0:T(8,128)(2,1)S(1)} %get-tuple-element.40) | copy-start | bytes 6291460
  82.4 1.1 copy-start.26
  91.2 1.0 copy-start.17
  94.5 80.6 %copy-start.4 = (f32[128,32]{1,0:T(8,128)S(1)}, f32[128,32]{1,0:T(8,128)}, u32[]{:S(2)}) copy-start(f32[128,32]{1,0:T(8,128)} %copy-done.3) | copy-start | bytes 49156
  170.0 100.8 %collective-permute-start = (bf16[2,2,128,1536]{3,2,1,0:T(8,128)(2,1)}, bf16[2,2,128,1536]{3,2,1,0:T(8,128)(2,1)S(1)}, u32[]{:S(2)}, u32[]{:S(2)}) collective-permute-start(bf16[2,2,128,1536]{3,2,1,0:T(8,128)(2,1)} %get-tuple-element.62), channel_id=1, source_target_pairs={{0,16},{16,32},{32,48},{48,0},{64,80},{80,96},{96,112},{112,64},{1... | collective-permute-start | bytes 4718600 | tf_op jit(solution)/shard_map/ppermute | solution.py:798
  171.8 99.0 %collective-permute-start.1 = (bf16[2,2,128,1536]{3,2,1,0:T(8,128)(2,1)}, bf16[2,2,128,1536]{3,2,1,0:T(8,128)(2,1)S(1)}, u32[]{:S(2)}, u32[]{:S(2)}) collective-permute-start(bf16[2,2,128,1536]{3,2,1,0:T(8,128)(2,1)} %get-tuple-element.63), channel_id=1, source_target_pairs={{0,32},{16,48},{32,0},{48,16},{64,96},{80,112},{96,64},{112,80},{1... | collective-permute-start | bytes 4718600 | tf_op jit(solution)/shard_map/ppermute | solution.py:798
  173.6 97.2 %collective-permute-start.2 = (bf16[2,2,128,1536]{3,2,1,0:T(8,128)(2,1)}, bf16[2,2,128,1536]{3,2,1,0:T(8,128)(2,1)S(1)}, u32[]{:S(2)}, u32[]{:S(2)}) collective-permute-start(bf16[2,2,128,1536]{3,2,1,0:T(8,128)(2,1)} %get-tuple-element.64), channel_id=1, source_target_pairs={{0,48},{16,0},{32,16},{48,32},{64,112},{80,64},{96,80},{112,96},{1... | collective-permute-start | bytes 4718600 | tf_op jit(solution)/shard_map/ppermute | solution.py:798
  175.1 1.0 copy-start.1
  176.1 1.0 copy-start.6
  177.2 1.2 copy-start.18
  178.4 1.0 copy-start.20
  179.4 1.0 copy-start.24
  180.4 0.9 copy-start.27
  197.8 1.6 copy-start.16
  199.4 63.1 %copy-start.2 = (f32[128,1024]{1,0:T(8,128)S(1)}, f32[128,1024]{1,0:T(8,128)}, u32[]{:S(2)}) copy-start(f32[128,1024]{1,0:T(8,128)} %copy-done) | copy-start | bytes 1572868
  199.4 63.1 %copy-start.7 = (f32[128,1024]{1,0:T(8,128)S(1)}, f32[128,1024]{1,0:T(8,128)}, u32[]{:S(2)}) copy-start(f32[128,1024]{1,0:T(8,128)} %copy-done.5) | copy-start | bytes 1572868
  199.4 63.1 %copy-start.10 = (bf16[1,128,1024]{2,1,0:T(8,128)(2,1)S(1)}, bf16[1,128,1024]{2,1,0:T(8,128)(2,1)}, u32[]{:S(2)}) copy-start(bf16[1,128,1024]{2,1,0:T(8,128)(2,1)} %param.12) | copy-start | bytes 786436
  199.4 63.2 %copy-start.15 = (bf16[1024,1024]{1,0:T(8,128)(2,1)S(1)}, bf16[1024,1024]{1,0:T(8,128)(2,1)}, u32[]{:S(2)}) copy-start(bf16[1024,1024]{1,0:T(8,128)(2,1)} %get-tuple-element.55.gwo) | copy-start | bytes 6291460
  199.4 63.2 %copy-start.21 = (f32[128,1024]{1,0:T(8,128)S(1)}, f32[128,1024]{1,0:T(8,128)}, u32[]{:S(2)}) copy-start(f32[128,1024]{1,0:T(8,128)} %copy-done.19) | copy-start | bytes 1572868
  199.4 63.2 %copy-start.23 = (bf16[128,1024]{1,0:T(8,128)(2,1)S(1)}, bf16[128,1024]{1,0:T(8,128)(2,1)}, u32[]{:S(2)}) copy-start(bf16[128,1024]{1,0:T(8,128)(2,1)} %copy-done.22) | copy-start | bytes 786436
  262.6 8.2 %copy-start.33 = (bf16[2,2,128,1536]{3,2,1,0:T(8,128)(2,1)S(1)}, bf16[2,2,128,1536]{3,2,1,0:T(8,128)(2,1)}, u32[]{:S(2)}) copy-start(bf16[2,2,128,1536]{3,2,1,0:T(8,128)(2,1)} %get-tuple-element.61) | copy-start | bytes 4718596
  271.6 1.7 copy-start.32
  271.7 61.5 %collective-permute-start.3 = (bf16[2,128,1536]{2,1,0:T(8,128)(2,1)S(1)}, bf16[2,128,1536]{2,1,0:T(8,128)(2,1)S(1)}, u32[]{:S(2)}, u32[]{:S(2)}) collective-permute-start(bf16[2,128,1536]{2,1,0:T(8,128)(2,1)S(1)} %fusion.1), channel_id=1, source_target_pairs={{0,64},{16,80},{32,96},{48,112},{64,0},{80,16},{96,32},{112,48},{1... | collective-permute-start | bytes 2359304 | tf_op jit(solution)/shard_map/ppermute | solution.py:800
  (6 other events, 4.9 us)
